TPU v7x, 32 devices: a whole 2x2x4 slice. The times are simulated.
32 devices in a mesh: aux: 16 (over z, y, x), occ: 2 (over core).
Axes of the slice: x: 2, y: 2, z: 4, core: 2. Of those that a mesh axis runs over, the one named last changes fastest.
Arguments:
- three_index: bfloat16 [64, 64, 64, 128], P('aux'), may hold values from -0.29882812 to 0.29882812
- coefficients: bfloat16 [5120, 256], P('aux', 'occ'), may hold values from -0.5 to 0.5
- row_blocks: int32 [64], P('aux'), may hold values from 0 to 15, as said below
- basis_blocks: int32 [64, 2], P('aux'), may hold values from 0 to 79, as said below
- fock_slot: int32 [112], replicated, may hold values from 0 to 111, as said below
Outputs:
- exchange: float32 [112, 4096], P('aux', 'occ')
Inputs may be any that keep to these rules, and one draw needn't show every extreme that they name: There is one offset c, the same for row_blocks and fock_slot: the 4 row blocks of aux index a are (a + c + s_j) mod 16 for j = 0..3, in order, with s_j = j * 4 for j < 3 and s_j = 15 for the last. `basis_blocks`: aux index a lists only basis blocks held by aux indices a - 1, a and a + 1 (cyclically, 5 blocks each, block b held by index b // 5); every aux index lists some block of a - 1 and some of a + 1. `fock_slot`: each position once; the 7 band blocks of row block r go, in some order, to positions ((r - c) mod 16) * 7 to ((r - c) mod 16) * 7 + 6, with the c of row_blocks.
All inputs are finite; a program needn't handle non-finite values.
Results may differ from a plain program's by a relative error of at most 0.00034.
Values may be sent and summed in bfloat16 or wider, within the bound.
No kernel may reach another device: no remote copies, remote signals or barrier semaphores. Data moves between devices by JAX's collectives and lax.ppermute only.
A program may use at most 64 MiB of HBM per device.

v0:
```python
import jax
import jax.numpy as jnp
from jax import lax
from jax.sharding import PartitionSpec as P


def padded(cells, sides, width):
    for axis, dim in sides:
        count = lax.axis_size(axis)
        head = lax.slice_in_dim(cells, 0, width, axis=dim)
        tail = lax.slice_in_dim(cells, cells.shape[dim] - width, cells.shape[dim], axis=dim)
        cells = jnp.concatenate(
            [
                lax.ppermute(tail, axis, [(i, (i + 1) % count) for i in range(count)]),
                cells,
                lax.ppermute(head, axis, [((i + 1) % count, i) for i in range(count)]),
            ],
            axis=dim,
        )
    return cells


def per_device(three_index, coefficients, row_blocks, basis_blocks, fock_slot):
    shard_rows = coefficients.shape[0]
    block_size = three_index.shape[2]
    entries = three_index.shape[0]
    per_entry = basis_blocks.shape[1]
    band_count = fock_slot.shape[0]
    band_width = 2 * entries - 1
    groups = lax.axis_size("aux")
    position = lax.axis_index("aux")
    nearby = padded(coefficients, (("aux", 0),), shard_rows)
    anchor = (position - 1) * shard_rows
    offsets = jnp.mod(basis_blocks * block_size - anchor, groups * shard_rows)

    def pick_rows(offset):
        return lax.dynamic_slice_in_dim(nearby, offset, block_size, 0)

    selected = jax.vmap(jax.vmap(pick_rows))(offsets)
    selected = selected.reshape(entries, per_entry * block_size, selected.shape[-1])
    halfway = jnp.einsum(
        "jpmk,jko->jpmo", three_index, selected, preferred_element_type=jnp.float32
    ).astype(jnp.bfloat16)
    partial_value = jnp.einsum(
        "jpmo,kpno->jkmn", halfway, halfway, preferred_element_type=jnp.float32
    )
    partial_value = partial_value.reshape(entries * entries, block_size * block_size)
    reduced = lax.psum_scatter(partial_value, "occ", scatter_dimension=1, tiled=True)
    entry_index = jnp.arange(entries, dtype=jnp.int32)
    offset_pair = entry_index[None, :] - entry_index[:, None] + entries - 1
    band_index = (row_blocks[:, None] * band_width + offset_pair).reshape(-1)
    column_ids = jnp.arange(band_count, dtype=jnp.int32)
    lookup = band_index[:, None] == column_ids[None, :]
    target = jnp.sum(jnp.where(lookup, fock_slot[None, :], 0), axis=1)
    placing = (target[:, None] == column_ids[None, :]).astype(jnp.float32)
    scattered = jnp.dot(
        placing.T, reduced, precision=lax.Precision.HIGHEST, preferred_element_type=jnp.float32
    )
    summed = lax.psum(scattered, "aux")
    owned = lax.dynamic_slice_in_dim(summed, position * band_width, band_width, 0)
    return owned


def solution(mesh):
    in_specs = (P("aux", None, None, None), P("aux", "occ"), P("aux"), P("aux", None), P())
    out_specs = P("aux", "occ")
    return jax.shard_map(
        per_device, mesh=mesh, in_specs=in_specs, out_specs=out_specs, check_vma=False
    )
```

profile of v0, /device:TPU:0, one launch (start us, length us, event | category | flops | bytes accessed | tf_op | source)
XLA Modules:
  0.0 172.4 jit_solution(15434783636929688715)
XLA Ops:
  6.5 0.0 reduce-scatter.2.cloned.1.call-start
  6.5 2.9 %collective-permute-start = (bf16[320,128]{1,0:T(8,128)(2,1)}, bf16[320,128]{1,0:T(8,128)(2,1)S(1)}, u32[]{:S(2)}, u32[]{:S(2)}) collective-permute-start(bf16[320,128]{1,0:T(8,128)(2,1)} %param.6), channel_id=1, source_target_pairs={{0,2},{2,4},{4,6},{6,8},{8,10},{10,12},{12,14},{14,16},{16,18},{18... | collective-permute-start | bytes 245768 | tf_op jit(solution)/shard_map/ppermute | solution.py:14
  9.5 4.0 %collective-permute-start.1 = (bf16[320,128]{1,0:T(8,128)(2,1)}, bf16[320,128]{1,0:T(8,128)(2,1)S(1)}, u32[]{:S(2)}, u32[]{:S(2)}) collective-permute-start(bf16[320,128]{1,0:T(8,128)(2,1)} %param.6), channel_id=1, source_target_pairs={{2,0},{4,2},{6,4},{8,6},{10,8},{12,10},{14,12},{16,14},{18,16},{20... | collective-permute-start | bytes 245768 | tf_op jit(solution)/shard_map/ppermute | solution.py:16
  13.5 0.7 fusion.13
  14.2 0.1 copy.14
  14.3 0.1 reshape.37
  14.4 1.9 %collective-permute-done = bf16[320,128]{1,0:T(8,128)(2,1)S(1)} collective-permute-done((bf16[320,128]{1,0:T(8,128)(2,1)}, bf16[320,128]{1,0:T(8,128)(2,1)S(1)}, u32[]{:S(2)}, u32[]{:S(2)}) %collective-permute-start) | collective-permute-done | bytes 81952 | tf_op jit(solution)/shard_map/ppermute | solution.py:14
  16.2 0.0 collective-permute-done.1
  16.2 0.9 pad_maximum_fusion
  17.1 10.6 %while.1 = (s32[]{:T(128)}, bf16[960,128]{1,0:T(8,128)(2,1)S(1)}, s32[8,2]{0,1:T(2,128)S(1)}, bf16[8,64,128]{2,1,0:T(8,128)(2,1)S(1)}, s32[]{:T(128)}) while((s32[]{:T(128)}, bf16[960,128]{1,0:T(8,128)(2,1)S(1)}, s32[8,2]{0,1:T(2,128)S(1)}, bf16[8,64,128]{2,1,0:T(8,128)(2,1)S(1)}, s32[]{:T(128)}) %tuple.16), condition=%wide.while_cond, body=%wide.while_body.sunk | while | flops 2 | bytes 32873 | solution.py:37
  17.1 0.1 constant_dynamic-slice_fusion.3
  17.2 0.6 slice.12
  17.8 0.7 bitcast_dynamic-update-slice_fusion.2
  18.5 0.1 constant_dynamic-slice_fusion.3
  18.5 0.6 slice.12
  19.1 0.7 bitcast_dynamic-update-slice_fusion.2
  19.8 0.1 constant_dynamic-slice_fusion.3
  19.9 0.6 slice.12
  20.4 0.7 bitcast_dynamic-update-slice_fusion.2
  21.1 0.1 constant_dynamic-slice_fusion.3
  21.2 0.6 slice.12
  21.8 0.7 bitcast_dynamic-update-slice_fusion.2
  22.4 0.1 constant_dynamic-slice_fusion.3
  22.5 0.6 slice.12
  23.1 0.7 bitcast_dynamic-update-slice_fusion.2
  23.8 0.1 constant_dynamic-slice_fusion.3
  23.8 0.6 slice.12
  24.4 0.7 bitcast_dynamic-update-slice_fusion.2
  25.1 0.1 constant_dynamic-slice_fusion.3
  25.2 0.6 slice.12
  25.7 0.7 bitcast_dynamic-update-slice_fusion.2
  26.4 0.1 constant_dynamic-slice_fusion.3
  26.5 0.6 slice.12
  27.1 0.7 bitcast_dynamic-update-slice_fusion.2
  27.7 0.0 copy-start
  27.7 0.0 copy-start.1
  27.8 7.9 %fusion.6 = f32[4,4,64,64]{2,3,0,1:T(8,128)S(1)} fusion(bf16[4,128,128,1]{2,1,3,0:T(8,128)(2,1)S(1)} %bitcast.41, bf16[4,64,64,128]{3,2,1,0:T(8,128)(2,1)} %param.5), kind=kOutput, calls=%fused_computation.7 | convolution fusion | flops 2151677952 | bytes 4587520 | tf_op jit(solution)/shard_map/jpmo,kpno->jkmn/dot_general | solution.py:44
  35.7 0.2 copy.10
  35.9 0.9 reshape.36
  36.8 0.0 reduce-scatter.2.cloned.1.call-update
  36.8 0.0 all-reduce.3.cloned.1.call-start
  36.9 0.0 copy-done
  36.9 0.1 add_add_fusion
  36.9 0.1 add.46
  37.0 0.0 copy-done.1
  37.0 0.2 select_reduce_fusion
  37.2 8.7 %reduce-scatter.2.cloned.1.call-done = f32[16,2048]{1,0:T(8,128)} async-done(((f32[16,4096]{1,0:T(8,128)}), f32[16,2048]{1,0:T(8,128)}) %reduce-scatter.2.cloned.1.call-update) | async-done | bytes 131088 | tf_op jit(solution)/shard_map/reduce_scatter | solution.py:48
  45.9 2.5 %fusion.11 = f32[112,2048]{1,0:T(8,128)} fusion(f32[16,2048]{1,0:T(8,128)} %reduce-scatter.2.cloned.1.call-done, s32[16]{0:T(128)S(1)} %select_reduce_fusion), kind=kOutput, calls=%fused_computation.12 | convolution fusion | flops 44041984 | bytes 1048640 | tf_op jit(solution)/shard_map/dot_general | solution.py:56
  48.3 0.0 all-reduce.3.cloned.1.call-update
  48.4 115.7 %all-reduce.3.cloned.1.call-done = f32[112,2048]{1,0:T(8,128)} async-done(((f32[112,2048]{1,0:T(8,128)}), f32[112,2048]{1,0:T(8,128)}) %all-reduce.3.cloned.1.call-update) | async-done | bytes 917520 | tf_op jit(solution)/shard_map/psum | solution.py:59
  164.0 1.5 constant_dynamic-slice_fusion.1
  (3 shorter events, 0.0 us)
Async XLA Ops:
  6.5 39.3 %reduce-scatter.2.cloned.1.call-start = ((), (), s32[]{:S(2)}) async-start(), calls=%async_computation.1 | async-start | bytes 393216 | tf_op jit(solution)/shard_map/reduce_scatter | solution.py:48
  6.5 9.7 %collective-permute-start = (bf16[320,128]{1,0:T(8,128)(2,1)}, bf16[320,128]{1,0:T(8,128)(2,1)S(1)}, u32[]{:S(2)}, u32[]{:S(2)}) collective-permute-start(bf16[320,128]{1,0:T(8,128)(2,1)} %param.6), channel_id=1, source_target_pairs={{0,2},{2,4},{4,6},{6,8},{8,10},{10,12},{12,14},{14,16},{16,18},{18... | collective-permute-start | bytes 245768 | tf_op jit(solution)/shard_map/ppermute | solution.py:14
  9.5 6.8 %collective-permute-start.1 = (bf16[320,128]{1,0:T(8,128)(2,1)}, bf16[320,128]{1,0:T(8,128)(2,1)S(1)}, u32[]{:S(2)}, u32[]{:S(2)}) collective-permute-start(bf16[320,128]{1,0:T(8,128)(2,1)} %param.6), channel_id=1, source_target_pairs={{2,0},{4,2},{6,4},{8,6},{10,8},{12,10},{14,12},{16,14},{18,16},{20... | collective-permute-start | bytes 245768 | tf_op jit(solution)/shard_map/ppermute | solution.py:16
  27.7 9.1 %copy-start = (s32[4]{0:T(128)S(1)}, s32[4]{0:T(128)}, u32[]{:S(2)}) copy-start(s32[4]{0:T(128)} %param.7) | copy-start | bytes 52
  27.7 9.3 %copy-start.1 = (s32[112]{0:T(128)S(1)}, s32[112]{0:T(128)}, u32[]{:S(2)}) copy-start(s32[112]{0:T(128)} %param.9) | copy-start | bytes 1348
  36.8 127.2 %all-reduce.3.cloned.1.call-start = ((), (), s32[]{:S(2)}) async-start(), calls=%async_computation.2 | async-start | bytes 1835008 | tf_op jit(solution)/shard_map/psum | solution.py:59
Sparse Core Ops, SparseCore 0:
  36.9 8.9 reduce-scatter.1
  52.0 111.9 all-reduce.2
where the time goes:
time: 173 us; the launch traced here: 172 us
  waiting for transfers between devices  126 us (73%)
  between operations  13.5 us (8%)
  local copies, waits for them, and re-layouts  13.3 us (8%)
  matrix products  10.4 us (6%)
  starting transfers between devices  6.98 us (4%)
  other arithmetic  1.85 us (1%)
    psum x1, waiting for transfers between devices, per_device(): summed = lax.psum(scattered, 'aux')  116 us
    gather x24, local copies, waits for them, and re-layouts  10.5 us
    reduce_scatter x1, waiting for transfers between devices, per_device(): lax.psum_scatter(partial_value, 'occ', scatter_dimension=1, tiled=True)  8.66 us
    dot_general x1, matrix products, per_device(): jnp.einsum('jpmo,kpno->jkmn', halfway, halfway, preferred_element_type=jn...  7.94 us
    ppermute x1, starting transfers between devices, padded(): lax.ppermute(head, axis, [((i + 1) % count, i) for i in range(count)])  4 us
  transfers between devices with their start and end apart: 4, of which 3 were waited for; matrix products, arithmetic and copies ran while one was open for 1% of the time, Pallas kernels for 0%

commit v1 on v0

v1 whole, which is shorter than its diff:
```python
import functools

import jax
import jax.numpy as jnp
from jax import lax
from jax.experimental import pallas as pl
from jax.experimental.pallas import tpu as pltpu
from jax.sharding import PartitionSpec as P

LANES = 128
CHUNK = 8
VMEM = pl.BlockSpec(memory_space=pltpu.VMEM)
SMEM = pl.BlockSpec(memory_space=pltpu.SMEM)


def build_kernel(groups, parts, blocks_ref, left_ref, own_ref, right_ref, three_ref, *rest):
    outs, (near, sel, half, acc, panels) = rest[:parts], rest[parts:]
    entries, aux_count, block, depth = three_ref.shape
    tiles = depth // block
    shard_rows, orbitals = own_ref.shape
    per_shard = shard_rows // block
    position = lax.axis_index("aux")
    lane = lax.axis_index("occ")

    near[0:shard_rows] = left_ref[...]
    near[shard_rows : 2 * shard_rows] = own_ref[...]
    near[2 * shard_rows : 3 * shard_rows] = right_ref[...]
    total = groups * per_shard
    for pair in range(entries // 2):
        sel[pair] = jnp.zeros(sel.shape[1:], sel.dtype)
    for e in range(entries):
        for t in range(tiles):
            offset = lax.rem(blocks_ref[e, t] - (position - 1) * per_shard + total, total)
            rows = near[pl.ds(pl.multiple_of(offset * block, block), block), :]
            at = (e % 2) * depth + t * block
            sel[e // 2, at : at + block, (e % 2) * orbitals : (e % 2 + 1) * orbitals] = rows

    acc[...] = jnp.zeros_like(acc)

    def step(s, carry):
        start = pl.multiple_of(s * CHUNK, CHUNK)
        for pair in range(entries // 2):
            lhs = jnp.concatenate(
                [three_ref[2 * pair + i, pl.ds(start, CHUNK)].reshape(CHUNK * block, depth) for i in range(2)], axis=1
            )
            res = jnp.dot(lhs, sel[pair], preferred_element_type=jnp.float32).astype(jnp.bfloat16)
            for i in range(2):
                e = 2 * pair + i
                for p in range(CHUNK):
                    half[e * block : (e + 1) * block, p * orbitals : (p + 1) * orbitals] = res[
                        p * block : (p + 1) * block, i * orbitals : (i + 1) * orbitals
                    ]
        full = half[...]
        acc[...] += lax.dot_general(full, full, (((1,), (1,)), ((), ())), preferred_element_type=jnp.float32)
        return carry

    lax.fori_loop(0, aux_count // CHUNK, step, 0)

    for h in range(entries // 2):
        panels[h] = acc[:, h * LANES : (h + 1) * LANES]
    count = block * block // parts // LANES
    low = lax.broadcasted_iota(jnp.int32, (count, LANES), 1) < block
    for r in range(parts):
        part = lax.rem(lane + r, parts)
        for j in range(entries):
            base = j * block + part * (block // parts)
            for k in range(0, entries, 2):
                even = panels[k // 2, pl.ds(base, count, stride=2), :]
                odd = panels[k // 2, pl.ds(base + 1, count, stride=2), :]
                outs[r][j, k] = jnp.where(low, even, pltpu.roll(odd, block, 1))
                outs[r][j, k + 1] = jnp.where(low, pltpu.roll(even, block, 1), odd)


def sum_kernel(parts, *refs):
    terms, outs = refs[:parts], refs[parts:]
    for j in range(len(outs)):
        value = terms[0][j]
        for term in terms[1:]:
            value = value + term[j]
        outs[j][...] = value


def place_kernel(slot_ref, row_ref, *refs):
    terms, out_ref, rows = refs[:-2], refs[-2], refs[-1]
    entries, _, count, _ = (len(terms),) + terms[0].shape
    band = 2 * entries - 1
    first = lax.axis_index("aux") * band
    row = row_ref[0] * band
    for off in range(band):
        value = None
        for j in range(entries):
            k = off - (entries - 1) + j
            if 0 <= k < entries:
                term = terms[j][k]
                value = term if value is None else value + term
        slot = slot_ref[row + off] - first
        rows[pl.ds(slot, count, stride=8), :] = value
    for c in range(count):
        out_ref[:, c * LANES : (c + 1) * LANES] = rows[c * 8 : c * 8 + band, :]


def per_device(three_index, coefficients, row_blocks, basis_blocks, fock_slot):
    entries, aux_count, block, depth = three_index.shape
    shard_rows, orbitals = coefficients.shape
    groups = lax.axis_size("aux")
    parts = lax.axis_size("occ")
    count = block * block // parts // LANES
    band = 2 * entries - 1

    def shift(value, axis, by):
        size = lax.axis_size(axis)
        return lax.ppermute(value, axis, [(i, (i + by) % size) for i in range(size)])

    left = shift(coefficients, "aux", 1)
    right = shift(coefficients, "aux", -1)
    pieces = pl.pallas_call(
        functools.partial(build_kernel, groups, parts),
        out_shape=[jax.ShapeDtypeStruct((entries, entries, count, LANES), jnp.float32)] * parts,
        in_specs=[SMEM, VMEM, VMEM, VMEM, VMEM],
        out_specs=[VMEM] * parts,
        scratch_shapes=[
            pltpu.VMEM((3 * shard_rows, orbitals), jnp.bfloat16),
            pltpu.VMEM((entries // 2, 2 * depth, 2 * orbitals), jnp.bfloat16),
            pltpu.VMEM((entries * block, CHUNK * orbitals), jnp.bfloat16),
            pltpu.VMEM((entries * block, entries * block), jnp.float32),
            pltpu.VMEM((entries // 2, entries * block, LANES), jnp.float32),
        ],
        compiler_params=pltpu.CompilerParams(vmem_limit_bytes=24 * 1024 * 1024),
    )(basis_blocks, left, coefficients, right, three_index)
    terms = [pieces[0]] + [shift(pieces[r], "occ", r) for r in range(1, parts)]
    rows = pl.pallas_call(
        functools.partial(sum_kernel, parts),
        out_shape=[jax.ShapeDtypeStruct((entries, count, LANES), jnp.float32)] * entries,
        in_specs=[VMEM] * parts,
        out_specs=[VMEM] * entries,
        compiler_params=pltpu.CompilerParams(vmem_limit_bytes=4 * 1024 * 1024),
    )(*terms)
    steps = [j * groups // entries for j in range(entries - 1)] + [groups - 1]
    moved = [rows[0]] + [shift(rows[j], "aux", steps[j]) for j in range(1, entries)]
    return pl.pallas_call(
        place_kernel,
        out_shape=jax.ShapeDtypeStruct((band, count * LANES), jnp.float32),
        in_specs=[SMEM, SMEM] + [VMEM] * entries,
        out_specs=VMEM,
        scratch_shapes=[pltpu.VMEM((count * 8, LANES), jnp.float32)],
        compiler_params=pltpu.CompilerParams(vmem_limit_bytes=4 * 1024 * 1024),
    )(fock_slot, row_blocks, *moved)


def solution(mesh):
    in_specs = (P("aux", None, None, None), P("aux", "occ"), P("aux"), P("aux", None), P())
    out_specs = P("aux", "occ")
    return jax.shard_map(
        per_device, mesh=mesh, in_specs=in_specs, out_specs=out_specs, check_vma=False
    )
```

time: 173 us -> 31.1 us (0.18)
  waiting for transfers between devices: 126 us -> 4.87 us
  between operations: 13.5 us -> 0.03 us
  matrix products: 10.4 us -> 0 us
  local copies, waits for them, and re-layouts: 13.3 us -> 3.85 us
  Pallas kernels: 0 us -> 7.94 us
  starting transfers between devices: 6.98 us -> 14.2 us
  other arithmetic: 1.85 us -> 0 us
    psum x1 -> x0, waiting for transfers between devices: 116 us -> none  [per_device(): summed = lax.psum(scattered, 'aux')]
    gather x24 -> x0, local copies, waits for them, and re-layouts: 10.5 us -> none
    dot_general x2 -> x0, matrix products: 10.4 us -> none  [the longest x1 7.94 us: per_device(): jnp.einsum('jpmo,kpno->jkmn', halfway, halfway, preferred_element_type=jn...]
    reduce_scatter x1 -> x0, waiting for transfers between devices: 8.66 us -> none  [per_device(): lax.psum_scatter(partial_value, 'occ', scatter_dimension=1, tiled=True)]
    pallas_call x0 -> x3, Pallas kernels: none -> 7.94 us  [the longest x1 6.73 us: per_device(): pl.pallas_call(functools.partial(build_kernel, groups, parts), out_shape=...]
    ppermute x2 -> x6, starting transfers between devices: 6.93 us -> 14.2 us  [shift(): lax.ppermute(value, axis, [(i, (i + by) % size) for i in range(size)])]
    unnamed x5 -> x9, local copies, waits for them, and re-layouts: 0.11 us -> 3.85 us
    ppermute x2 -> x6, waiting for transfers between devices: 1.87 us -> 4.87 us  [shift(): lax.ppermute(value, axis, [(i, (i + by) % size) for i in range(size)])]
  transfers between devices with their start and end apart: 4 -> 6, of which waited for: 3 -> 3; matrix products, arithmetic and copies ran while one was open for 1% -> 2% of each run, Pallas kernels for 0% -> 0%
where the time goes in v1:
time: 31.1 us; the launch traced here: 30.9 us
  starting transfers between devices  14.2 us (46%)
  Pallas kernels  7.94 us (26%)
  waiting for transfers between devices  4.87 us (16%)
  local copies, waits for them, and re-layouts  3.85 us (12%)
    ppermute x6, starting transfers between devices, shift(): lax.ppermute(value, axis, [(i, (i + by) % size) for i in range(size)])  14.2 us
    pallas_call x1, Pallas kernels, per_device(): pl.pallas_call(functools.partial(build_kernel, groups, parts), out_shape=...  6.73 us
    ppermute x6, waiting for transfers between devices, shift(): lax.ppermute(value, axis, [(i, (i + by) % size) for i in range(size)])  4.87 us
    unnamed x9, local copies, waits for them, and re-layouts  3.85 us
    pallas_call x1, Pallas kernels, per_device(): pl.pallas_call(place_kernel, out_shape=jax.ShapeDtypeStruct((band, count...  1.2 us
  transfers between devices with their start and end apart: 6, of which 3 were waited for; matrix products, arithmetic and copies ran while one was open for 2% of the time, Pallas kernels for 0%

profile of v1, /device:TPU:0, one launch (start us, length us, event | category | flops | bytes accessed | tf_op | source)
XLA Modules:
  0.0 30.9 jit_solution(18006891052758270748)
XLA Ops:
  0.0 0.0 copy-start.2
  0.0 0.0 copy-start.3
  0.0 2.9 %collective-permute-start = (bf16[320,128]{1,0:T(8,128)(2,1)}, bf16[320,128]{1,0:T(8,128)(2,1)S(1)}, u32[]{:S(2)}, u32[]{:S(2)}) collective-permute-start(bf16[320,128]{1,0:T(8,128)(2,1)} %own_ref.1), channel_id=1, source_target_pairs={{0,2},{2,4},{4,6},{6,8},{8,10},{10,12},{12,14},{14,16},{16,18},{18... | collective-permute-start | bytes 245768 | tf_op jit(solution)/shard_map/ppermute | solution.py:112
  2.9 4.1 %collective-permute-start.1 = (bf16[320,128]{1,0:T(8,128)(2,1)}, bf16[320,128]{1,0:T(8,128)(2,1)S(1)}, u32[]{:S(2)}, u32[]{:S(2)}) collective-permute-start(bf16[320,128]{1,0:T(8,128)(2,1)} %own_ref.1), channel_id=1, source_target_pairs={{0,30},{2,0},{4,2},{6,4},{8,6},{10,8},{12,10},{14,12},{16,14},{18,... | collective-permute-start | bytes 245768 | tf_op jit(solution)/shard_map/ppermute | solution.py:112
  7.0 0.8 %copy.6.blocks_ref = s32[4,2]{1,0:T(4,128)S(1)} copy(s32[4,2]{0,1:T(2,128)} %param.8) | data formatting | bytes 64 | tf_op args[3]
  7.8 1.9 %collective-permute-done.left_ref = bf16[320,128]{1,0:T(8,128)(2,1)S(1)} collective-permute-done((bf16[320,128]{1,0:T(8,128)(2,1)}, bf16[320,128]{1,0:T(8,128)(2,1)S(1)}, u32[]{:S(2)}, u32[]{:S(2)}) %collective-permute-start) | collective-permute-done | bytes 81952 | tf_op jit(solution)/shard_map/ppermute | solution.py:112
  9.7 0.0 collective-permute-done.1.right_ref
  9.7 0.0 copy-start
  9.7 2.2 %copy-done = bf16[4,64,64,128]{3,2,1,0:T(8,128)(2,1)S(1)} copy-done((bf16[4,64,64,128]{3,2,1,0:T(8,128)(2,1)S(1)}, bf16[4,64,64,128]{3,2,1,0:T(8,128)(2,1)}, u32[]{:S(2)}) %copy-start) | copy-done | bytes 4194328
  11.9 0.0 copy-start.1
  11.9 0.9 %copy-done.1 = bf16[320,128]{1,0:T(8,128)(2,1)S(1)} copy-done((bf16[320,128]{1,0:T(8,128)(2,1)S(1)}, bf16[320,128]{1,0:T(8,128)(2,1)}, u32[]{:S(2)}) %copy-start.1) | copy-done | bytes 81944
  12.8 6.7 %shard_map.55 = (f32[4,4,16,128]{3,2,1,0:T(8,128)S(1)}, f32[4,4,16,128]{3,2,1,0:T(8,128)S(1)}) custom-call(s32[4,2]{1,0:T(4,128)S(1)} %copy.6.blocks_ref, bf16[320,128]{1,0:T(8,128)(2,1)S(1)} %collective-permute-done.left_ref, bf16[320,128]{1,0:T(8,128)(2,1)S(1)} %copy-done.1, bf16[320,128]{1,0:T(8,128)(2,1)S(1)} %collective-permute-done.1.right_ref, ...), custom_call_target="tpu_custom_call" | custom-call | tf_op jit(solution)/shard_map/pallas_call | solution.py:116
  19.5 0.1 collective-permute-start.2
  19.6 1.3 %collective-permute-done.2.refs_1_ = f32[4,4,16,128]{3,2,1,0:T(8,128)S(1)} collective-permute-done((f32[4,4,16,128]{3,2,1,0:T(8,128)S(1)}, f32[4,4,16,128]{3,2,1,0:T(8,128)S(1)}, u32[]{:S(2)}, u32[]{:S(2)}) %collective-permute-start.2) | collective-permute-done | bytes 131104 | tf_op jit(solution)/shard_map/ppermute | solution.py:112
  20.9 0.5 %collective-permute-start.3 = (f32[4,16,128]{2,1,0:T(8,128)S(1)}, f32[4,16,128]{2,1,0:T(8,128)S(1)}, u32[]{:S(2)}, u32[]{:S(2)}) collective-permute-start(f32[4,16,128]{2,1,0:T(8,128)S(1)} %get-tuple-element.14), channel_id=1, source_target_pairs={{0,8},{2,10},{4,12},{6,14},{8,16},{10,18},{12,20},{14,22},{16,24},... | collective-permute-start | bytes 98312 | tf_op jit(solution)/shard_map/ppermute | solution.py:112
  21.4 2.6 %collective-permute-start.4 = (f32[4,16,128]{2,1,0:T(8,128)S(1)}, f32[4,16,128]{2,1,0:T(8,128)S(1)}, u32[]{:S(2)}, u32[]{:S(2)}) collective-permute-start(f32[4,16,128]{2,1,0:T(8,128)S(1)} %get-tuple-element.15), channel_id=1, source_target_pairs={{0,16},{2,18},{4,20},{6,22},{8,24},{10,26},{12,28},{14,30},{16,0},... | collective-permute-start | bytes 98312 | tf_op jit(solution)/shard_map/ppermute | solution.py:112
  24.0 4.1 %collective-permute-start.5 = (f32[4,16,128]{2,1,0:T(8,128)S(1)}, f32[4,16,128]{2,1,0:T(8,128)S(1)}, u32[]{:S(2)}, u32[]{:S(2)}) collective-permute-start(f32[4,16,128]{2,1,0:T(8,128)S(1)} %get-tuple-element.16), channel_id=1, source_target_pairs={{0,30},{2,0},{4,2},{6,4},{8,6},{10,8},{12,10},{14,12},{16,14},{18,... | collective-permute-start | bytes 98312 | tf_op jit(solution)/shard_map/ppermute | solution.py:112
  28.1 0.0 collective-permute-done.3.refs_1_
  28.1 0.0 collective-permute-done.4.refs_2_
  28.1 1.6 %collective-permute-done.5.refs_3_ = f32[4,16,128]{2,1,0:T(8,128)S(1)} collective-permute-done((f32[4,16,128]{2,1,0:T(8,128)S(1)}, f32[4,16,128]{2,1,0:T(8,128)S(1)}, u32[]{:S(2)}, u32[]{:S(2)}) %collective-permute-start.5) | collective-permute-done | bytes 32800 | tf_op jit(solution)/shard_map/ppermute | solution.py:112
  29.7 0.0 copy-done.2
  29.7 0.0 copy-done.3
  29.7 1.2 %shard_map.57 = f32[7,2048]{1,0:T(8,128)} custom-call(s32[112]{0:T(128)S(1)} %copy-done.2, s32[4]{0:T(128)S(1)} %copy-done.3, f32[4,16,128]{2,1,0:T(8,128)S(1)} %get-tuple-element.13.refs_0_, f32[4,16,128]{2,1,0:T(8,128)S(1)} %collective-permute-done.3.refs_1_, f32[4,16,128]{2,1,0:T(8,128)S(1)} %collective-permute-done.4.refs_2_, ...), custom_call_target="tpu_custom_call" | custom-call | tf_op jit(solution)/shard_map/pallas_call | solution.py:140
  (1 shorter events, 0.0 us)
Async XLA Ops:
  0.0 29.7 %copy-start.2 = (s32[112]{0:T(128)S(1)}, s32[112]{0:T(128)}, u32[]{:S(2)}) copy-start(s32[112]{0:T(128)} %slot_ref.1) | copy-start | bytes 1348
  0.0 29.7 %copy-start.3 = (s32[4]{0:T(128)S(1)}, s32[4]{0:T(128)}, u32[]{:S(2)}) copy-start(s32[4]{0:T(128)} %row_ref.1) | copy-start | bytes 52
  0.0 9.7 %collective-permute-start = (bf16[320,128]{1,0:T(8,128)(2,1)}, bf16[320,128]{1,0:T(8,128)(2,1)S(1)}, u32[]{:S(2)}, u32[]{:S(2)}) collective-permute-start(bf16[320,128]{1,0:T(8,128)(2,1)} %own_ref.1), channel_id=1, source_target_pairs={{0,2},{2,4},{4,6},{6,8},{8,10},{10,12},{12,14},{14,16},{16,18},{18... | collective-permute-start | bytes 245768 | tf_op jit(solution)/shard_map/ppermute | solution.py:112
  2.9 6.8 %collective-permute-start.1 = (bf16[320,128]{1,0:T(8,128)(2,1)}, bf16[320,128]{1,0:T(8,128)(2,1)S(1)}, u32[]{:S(2)}, u32[]{:S(2)}) collective-permute-start(bf16[320,128]{1,0:T(8,128)(2,1)} %own_ref.1), channel_id=1, source_target_pairs={{0,30},{2,0},{4,2},{6,4},{8,6},{10,8},{12,10},{14,12},{16,14},{18,... | collective-permute-start | bytes 245768 | tf_op jit(solution)/shard_map/ppermute | solution.py:112
  9.7 2.2 %copy-start = (bf16[4,64,64,128]{3,2,1,0:T(8,128)(2,1)S(1)}, bf16[4,64,64,128]{3,2,1,0:T(8,128)(2,1)}, u32[]{:S(2)}) copy-start(bf16[4,64,64,128]{3,2,1,0:T(8,128)(2,1)} %three_ref.1) | copy-start | bytes 12582916
  11.9 0.9 %copy-start.1 = (bf16[320,128]{1,0:T(8,128)(2,1)S(1)}, bf16[320,128]{1,0:T(8,128)(2,1)}, u32[]{:S(2)}) copy-start(bf16[320,128]{1,0:T(8,128)(2,1)} %own_ref.1) | copy-start | bytes 245764
  19.5 1.4 %collective-permute-start.2 = (f32[4,4,16,128]{3,2,1,0:T(8,128)S(1)}, f32[4,4,16,128]{3,2,1,0:T(8,128)S(1)}, u32[]{:S(2)}, u32[]{:S(2)}) collective-permute-start(f32[4,4,16,128]{3,2,1,0:T(8,128)S(1)} %get-tuple-element.12), channel_id=1, source_target_pairs={{0,1},{1,0},{2,3},{3,2},{4,5},{5,4},{6,7},{7,6},{8,9},{9,8},{10,11... | collective-permute-start | bytes 393224 | tf_op jit(solution)/shard_map/ppermute | solution.py:112
  20.9 7.1 %collective-permute-start.3 = (f32[4,16,128]{2,1,0:T(8,128)S(1)}, f32[4,16,128]{2,1,0:T(8,128)S(1)}, u32[]{:S(2)}, u32[]{:S(2)}) collective-permute-start(f32[4,16,128]{2,1,0:T(8,128)S(1)} %get-tuple-element.14), channel_id=1, source_target_pairs={{0,8},{2,10},{4,12},{6,14},{8,16},{10,18},{12,20},{14,22},{16,24},... | collective-permute-start | bytes 98312 | tf_op jit(solution)/shard_map/ppermute | solution.py:112
  21.4 6.7 %collective-permute-start.4 = (f32[4,16,128]{2,1,0:T(8,128)S(1)}, f32[4,16,128]{2,1,0:T(8,128)S(1)}, u32[]{:S(2)}, u32[]{:S(2)}) collective-permute-start(f32[4,16,128]{2,1,0:T(8,128)S(1)} %get-tuple-element.15), channel_id=1, source_target_pairs={{0,16},{2,18},{4,20},{6,22},{8,24},{10,26},{12,28},{14,30},{16,0},... | collective-permute-start | bytes 98312 | tf_op jit(solution)/shard_map/ppermute | solution.py:112
  24.0 5.7 %collective-permute-start.5 = (f32[4,16,128]{2,1,0:T(8,128)S(1)}, f32[4,16,128]{2,1,0:T(8,128)S(1)}, u32[]{:S(2)}, u32[]{:S(2)}) collective-permute-start(f32[4,16,128]{2,1,0:T(8,128)S(1)} %get-tuple-element.16), channel_id=1, source_target_pairs={{0,30},{2,0},{4,2},{6,4},{8,6},{10,8},{12,10},{14,12},{16,14},{18,... | collective-permute-start | bytes 98312 | tf_op jit(solution)/shard_map/ppermute | solution.py:112

commit v2 on v1

--- a/solution.py
+++ b/solution.py
@@ -8,12 +8,18 @@
 from jax.sharding import PartitionSpec as P
 
 LANES = 128
-CHUNK = 8
+CHUNK = 16
 VMEM = pl.BlockSpec(memory_space=pltpu.VMEM)
 SMEM = pl.BlockSpec(memory_space=pltpu.SMEM)
 
 
-def build_kernel(groups, parts, blocks_ref, left_ref, own_ref, right_ref, three_ref, *rest):
+def fetch_kernel(source, target, sem):
+    copy = pltpu.make_async_copy(source, target, sem)
+    copy.start()
+    copy.wait()
+
+
+def build_kernel(groups, parts, blocks_ref, far_ref, own_ref, near_ref, three_ref, *rest):
     outs, (near, sel, half, acc, panels) = rest[:parts], rest[parts:]
     entries, aux_count, block, depth = three_ref.shape
     tiles = depth // block
@@ -22,16 +28,22 @@
     position = lax.axis_index("aux")
     lane = lax.axis_index("occ")
 
-    near[0:shard_rows] = left_ref[...]
+    offset = lax.rem(blocks_ref[...] - (position - 1) * per_shard + groups * per_shard, groups * per_shard)
+    side, within = lax.div(offset, per_shard), lax.rem(offset, per_shard)
+    offsets = (jnp.where(lax.rem(position, 2) == 0, side, 2 - side) * per_shard + within).astype(jnp.float32)
+    tile_at = lax.broadcasted_iota(jnp.int32, offsets.shape, 0)
+    entry_at = lax.broadcasted_iota(jnp.int32, offsets.shape, 1)
+
+    near[0:shard_rows] = far_ref[...]
     near[shard_rows : 2 * shard_rows] = own_ref[...]
-    near[2 * shard_rows : 3 * shard_rows] = right_ref[...]
-    total = groups * per_shard
+    near[2 * shard_rows : 3 * shard_rows] = near_ref[...]
     for pair in range(entries // 2):
         sel[pair] = jnp.zeros(sel.shape[1:], sel.dtype)
     for e in range(entries):
         for t in range(tiles):
-            offset = lax.rem(blocks_ref[e, t] - (position - 1) * per_shard + total, total)
-            rows = near[pl.ds(pl.multiple_of(offset * block, block), block), :]
+            mine = (tile_at == t) & (entry_at == e)
+            offset = jnp.max(jnp.where(mine, offsets, 0.0)).astype(jnp.int32) * block
+            rows = near[pl.ds(pl.multiple_of(offset, block), block), :]
             at = (e % 2) * depth + t * block
             sel[e // 2, at : at + block, (e % 2) * orbitals : (e % 2 + 1) * orbitals] = rows
 
@@ -54,7 +66,7 @@
         acc[...] += lax.dot_general(full, full, (((1,), (1,)), ((), ())), preferred_element_type=jnp.float32)
         return carry
 
-    lax.fori_loop(0, aux_count // CHUNK, step, 0)
+    lax.fori_loop(0, aux_count // CHUNK, step, 0, unroll=True)
 
     for h in range(entries // 2):
         panels[h] = acc[:, h * LANES : (h + 1) * LANES]
@@ -80,12 +92,10 @@
         outs[j][...] = value
 
 
-def place_kernel(slot_ref, row_ref, *refs):
+def place_kernel(slot_ref, *refs):
     terms, out_ref, rows = refs[:-2], refs[-2], refs[-1]
-    entries, _, count, _ = (len(terms),) + terms[0].shape
+    entries, count = len(terms), terms[0].shape[1]
     band = 2 * entries - 1
-    first = lax.axis_index("aux") * band
-    row = row_ref[0] * band
     for off in range(band):
         value = None
         for j in range(entries):
@@ -93,10 +103,15 @@
             if 0 <= k < entries:
                 term = terms[j][k]
                 value = term if value is None else value + term
-        slot = slot_ref[row + off] - first
-        rows[pl.ds(slot, count, stride=8), :] = value
+        rows[pl.ds(off, count, stride=8), :] = value
+    shape = (8, slot_ref.shape[1])
+    lines = lax.broadcasted_iota(jnp.int32, shape, 0) + lax.axis_index("aux") * band
+    offs = lax.rem(lax.broadcasted_iota(jnp.int32, shape, 1), band).astype(jnp.float32)
+    order = jnp.sum(jnp.where(slot_ref[...] == lines, offs, 0.0), axis=1, keepdims=True).astype(jnp.int32)
+    order = jnp.broadcast_to(jnp.minimum(order, 7), (8, LANES))
     for c in range(count):
-        out_ref[:, c * LANES : (c + 1) * LANES] = rows[c * 8 : c * 8 + band, :]
+        placed = jnp.take_along_axis(rows[c * 8 : c * 8 + 8, :], order, axis=0, mode="promise_in_bounds")
+        out_ref[:, c * LANES : (c + 1) * LANES] = placed[:band]
 
 
 def per_device(three_index, coefficients, row_blocks, basis_blocks, fock_slot):
@@ -111,12 +126,24 @@
         size = lax.axis_size(axis)
         return lax.ppermute(value, axis, [(i, (i + by) % size) for i in range(size)])
 
-    left = shift(coefficients, "aux", 1)
-    right = shift(coefficients, "aux", -1)
+    def swap(value, first):
+        pairs = [((i + first) % groups, (i + first + 1) % groups) for i in range(0, groups, 2)]
+        return lax.ppermute(value, "aux", pairs + [(b, a) for a, b in pairs])
+
+    neighbour = swap(coefficients, 0)
+    other = swap(coefficients, 1)
+    held = pl.pallas_call(
+        fetch_kernel,
+        out_shape=jax.ShapeDtypeStruct(three_index.shape, three_index.dtype),
+        in_specs=[pl.BlockSpec(memory_space=pl.ANY)],
+        out_specs=VMEM,
+        scratch_shapes=[pltpu.SemaphoreType.DMA],
+        compiler_params=pltpu.CompilerParams(vmem_limit_bytes=8 * 1024 * 1024),
+    )(three_index)
     pieces = pl.pallas_call(
         functools.partial(build_kernel, groups, parts),
         out_shape=[jax.ShapeDtypeStruct((entries, entries, count, LANES), jnp.float32)] * parts,
-        in_specs=[SMEM, VMEM, VMEM, VMEM, VMEM],
+        in_specs=[VMEM] * 5,
         out_specs=[VMEM] * parts,
         scratch_shapes=[
             pltpu.VMEM((3 * shard_rows, orbitals), jnp.bfloat16),
@@ -125,8 +152,8 @@
             pltpu.VMEM((entries * block, entries * block), jnp.float32),
             pltpu.VMEM((entries // 2, entries * block, LANES), jnp.float32),
         ],
-        compiler_params=pltpu.CompilerParams(vmem_limit_bytes=24 * 1024 * 1024),
-    )(basis_blocks, left, coefficients, right, three_index)
+        compiler_params=pltpu.CompilerParams(vmem_limit_bytes=12 * 1024 * 1024),
+    )(basis_blocks.T, other, coefficients, neighbour, held)
     terms = [pieces[0]] + [shift(pieces[r], "occ", r) for r in range(1, parts)]
     rows = pl.pallas_call(
         functools.partial(sum_kernel, parts),
@@ -140,11 +167,11 @@
     return pl.pallas_call(
         place_kernel,
         out_shape=jax.ShapeDtypeStruct((band, count * LANES), jnp.float32),
-        in_specs=[SMEM, SMEM] + [VMEM] * entries,
+        in_specs=[VMEM] * (entries + 1),
         out_specs=VMEM,
         scratch_shapes=[pltpu.VMEM((count * 8, LANES), jnp.float32)],
         compiler_params=pltpu.CompilerParams(vmem_limit_bytes=4 * 1024 * 1024),
-    )(fock_slot, row_blocks, *moved)
+    )(fock_slot.reshape(1, -1), *moved)
 
 
 def solution(mesh):

time: 31.1 us -> 23.6 us (0.76)
  Pallas kernels: 7.94 us -> 4.14 us
  starting transfers between devices: 14.2 us -> 10.8 us
  local copies, waits for them, and re-layouts: 3.85 us -> 2.2 us
  waiting for transfers between devices: 4.87 us -> 6.14 us
    ppermute x6 -> x4, starting transfers between devices: 14.2 us -> 3.9 us  [shift(): lax.ppermute(value, axis, [(i, (i + by) % size) for i in range(size)])]
    ppermute x0 -> x2, starting transfers between devices: none -> 6.93 us  [swap(): return lax.ppermute(value, 'aux', pairs + [(b, a) for a, b in pairs])]
    pallas_call x1, Pallas kernels: 6.73 us -> 3.11 us  [per_device(): pl.pallas_call(functools.partial(build_kernel, groups, parts), out_shape=...]
    ppermute x0 -> x2, waiting for transfers between devices: none -> 2.15 us  [swap(): return lax.ppermute(value, 'aux', pairs + [(b, a) for a, b in pairs])]
    unnamed x9 -> x8, local copies, waits for them, and re-layouts: 3.85 us -> 2.2 us
    ppermute x6 -> x4, waiting for transfers between devices: 4.87 us -> 3.99 us  [shift(): lax.ppermute(value, axis, [(i, (i + by) % size) for i in range(size)])]
    pallas_call x1, Pallas kernels: 1.2 us -> 0.73 us  [per_device(): pl.pallas_call(place_kernel, out_shape=jax.ShapeDtypeStruct((band, count...]
  transfers between devices with their start and end apart: 6 -> 6, of which waited for: 3 -> 5; matrix products, arithmetic and copies ran while one was open for 2% -> 0% of each run, Pallas kernels for 0% -> 1%
where the time goes in v2:
time: 23.6 us; the launch traced here: 23.4 us
  starting transfers between devices  10.8 us (46%)
  waiting for transfers between devices  6.14 us (26%)
  Pallas kernels  4.14 us (18%)
  local copies, waits for them, and re-layouts  2.2 us (9%)
    ppermute x2, starting transfers between devices, swap(): return lax.ppermute(value, 'aux', pairs + [(b, a) for a, b in pairs])  6.93 us
    ppermute x4, waiting for transfers between devices, shift(): lax.ppermute(value, axis, [(i, (i + by) % size) for i in range(size)])  3.99 us
    ppermute x4, starting transfers between devices, shift(): lax.ppermute(value, axis, [(i, (i + by) % size) for i in range(size)])  3.9 us
    pallas_call x1, Pallas kernels, per_device(): pl.pallas_call(functools.partial(build_kernel, groups, parts), out_shape=...  3.11 us
    unnamed x8, local copies, waits for them, and re-layouts  2.2 us
    ppermute x2, waiting for transfers between devices, swap(): return lax.ppermute(value, 'aux', pairs + [(b, a) for a, b in pairs])  2.15 us
    pallas_call x1, Pallas kernels, per_device(): pl.pallas_call(place_kernel, out_shape=jax.ShapeDtypeStruct((band, count...  0.73 us
  transfers between devices with their start and end apart: 6, of which 5 were waited for; matrix products, arithmetic and copies ran while one was open for 0% of the time, Pallas kernels for 1%

profile of v2, /device:TPU:0, one launch (start us, length us, event | category | flops | bytes accessed | tf_op | source)
XLA Modules:
  0.0 23.4 jit_solution(1548863424671818804)
XLA Ops:
  0.0 6.9 %collective-permute-start = (bf16[320,128]{1,0:T(8,128)(2,1)}, bf16[320,128]{1,0:T(8,128)(2,1)S(1)}, u32[]{:S(2)}, u32[]{:S(2)}) collective-permute-start(bf16[320,128]{1,0:T(8,128)(2,1)} %own_ref.1), channel_id=1, source_target_pairs={{2,4},{6,8},{10,12},{14,16},{18,20},{22,24},{26,28},{30,0},{4,2},{... | collective-permute-start | bytes 245768 | tf_op jit(solution)/shard_map/ppermute | solution.py:131
  6.9 0.0 collective-permute-start.1
  6.9 0.0 copy-start
  6.9 2.2 %copy-done = bf16[4,64,64,128]{3,2,1,0:T(8,128)(2,1)S(1)} copy-done((bf16[4,64,64,128]{3,2,1,0:T(8,128)(2,1)S(1)}, bf16[4,64,64,128]{3,2,1,0:T(8,128)(2,1)}, u32[]{:S(2)}) %copy-start) | copy-done | bytes 4194328
  9.1 0.0 copy-start.1
  9.1 0.0 copy-start.2
  9.1 0.3 %shard_map.46.three_ref = bf16[4,64,64,128]{3,2,1,0:T(8,128)(2,1)S(1)} custom-call(bf16[4,64,64,128]{3,2,1,0:T(8,128)(2,1)S(1)} %copy-done), custom_call_target="tpu_custom_call" | custom-call | tf_op jit(solution)/shard_map/pallas_call | solution.py:135
  9.4 0.0 copy-start.3
  9.4 0.3 %collective-permute-done.far_ref = bf16[320,128]{1,0:T(8,128)(2,1)S(1)} collective-permute-done((bf16[320,128]{1,0:T(8,128)(2,1)}, bf16[320,128]{1,0:T(8,128)(2,1)S(1)}, u32[]{:S(2)}, u32[]{:S(2)}) %collective-permute-start) | collective-permute-done | bytes 81952 | tf_op jit(solution)/shard_map/ppermute | solution.py:131
  9.7 1.9 %collective-permute-done.1.near_ref = bf16[320,128]{1,0:T(8,128)(2,1)S(1)} collective-permute-done((bf16[320,128]{1,0:T(8,128)(2,1)}, bf16[320,128]{1,0:T(8,128)(2,1)S(1)}, u32[]{:S(2)}, u32[]{:S(2)}) %collective-permute-start.1) | collective-permute-done | bytes 81952 | tf_op jit(solution)/shard_map/ppermute | solution.py:131
  11.6 0.0 copy-done.1
  11.6 0.0 copy-done.2
  11.6 3.1 %shard_map.47 = (f32[4,4,16,128]{3,2,1,0:T(8,128)S(1)}, f32[4,4,16,128]{3,2,1,0:T(8,128)S(1)}) custom-call(s32[2,4]{1,0:T(2,128)S(1)} %bitcast.2, bf16[320,128]{1,0:T(8,128)(2,1)S(1)} %collective-permute-done.far_ref, bf16[320,128]{1,0:T(8,128)(2,1)S(1)} %copy-done.1, bf16[320,128]{1,0:T(8,128)(2,1)S(1)} %collective-permute-done.1.near_ref, ...), custom_call_target="tpu_custom_call" | custom-call | tf_op jit(solution)/shard_map/pallas_call | solution.py:143
  14.7 0.1 collective-permute-start.2
  14.8 1.3 %collective-permute-done.2.refs_1_ = f32[4,4,16,128]{3,2,1,0:T(8,128)S(1)} collective-permute-done((f32[4,4,16,128]{3,2,1,0:T(8,128)S(1)}, f32[4,4,16,128]{3,2,1,0:T(8,128)S(1)}, u32[]{:S(2)}, u32[]{:S(2)}) %collective-permute-start.2) | collective-permute-done | bytes 131104 | tf_op jit(solution)/shard_map/ppermute | solution.py:127
  16.1 0.1 collective-permute-start.3
  16.2 1.3 %collective-permute-start.4 = (f32[4,16,128]{2,1,0:T(8,128)S(1)}, f32[4,16,128]{2,1,0:T(8,128)S(1)}, u32[]{:S(2)}, u32[]{:S(2)}) collective-permute-start(f32[4,16,128]{2,1,0:T(8,128)S(1)} %get-tuple-element.15), channel_id=1, source_target_pairs={{0,16},{2,18},{4,20},{6,22},{8,24},{10,26},{12,28},{14,30},{16,0},... | collective-permute-start | bytes 98312 | tf_op jit(solution)/shard_map/ppermute | solution.py:127
  17.5 2.4 %collective-permute-start.5 = (f32[4,16,128]{2,1,0:T(8,128)S(1)}, f32[4,16,128]{2,1,0:T(8,128)S(1)}, u32[]{:S(2)}, u32[]{:S(2)}) collective-permute-start(f32[4,16,128]{2,1,0:T(8,128)S(1)} %get-tuple-element.16), channel_id=1, source_target_pairs={{0,30},{2,0},{4,2},{6,4},{8,6},{10,8},{12,10},{14,12},{16,14},{18,... | collective-permute-start | bytes 98312 | tf_op jit(solution)/shard_map/ppermute | solution.py:127
  20.0 1.9 %collective-permute-done.3.refs_1_ = f32[4,16,128]{2,1,0:T(8,128)S(1)} collective-permute-done((f32[4,16,128]{2,1,0:T(8,128)S(1)}, f32[4,16,128]{2,1,0:T(8,128)S(1)}, u32[]{:S(2)}, u32[]{:S(2)}) %collective-permute-start.3) | collective-permute-done | bytes 32800 | tf_op jit(solution)/shard_map/ppermute | solution.py:127
  21.9 0.7 %collective-permute-done.4.refs_2_ = f32[4,16,128]{2,1,0:T(8,128)S(1)} collective-permute-done((f32[4,16,128]{2,1,0:T(8,128)S(1)}, f32[4,16,128]{2,1,0:T(8,128)S(1)}, u32[]{:S(2)}, u32[]{:S(2)}) %collective-permute-start.4) | collective-permute-done | bytes 32800 | tf_op jit(solution)/shard_map/ppermute | solution.py:127
  22.6 0.0 collective-permute-done.5.refs_3_
  22.6 0.0 copy-done.3
  22.6 0.7 %shard_map.49 = f32[7,2048]{1,0:T(8,128)} custom-call(s32[1,112]{1,0:T(1,128)S(1)} %bitcast.3, f32[4,16,128]{2,1,0:T(8,128)S(1)} %get-tuple-element.13.refs_0_, f32[4,16,128]{2,1,0:T(8,128)S(1)} %collective-permute-done.3.refs_1_, f32[4,16,128]{2,1,0:T(8,128)S(1)} %collective-permute-done.4.refs_2_, f32[4,16,128]{2,1,0:T(8,128)S(1)} %collective-permute-done.5.refs_3_), custom_call_target="tpu_custom_call" | custom-call | tf_op jit(solution)/shard_map/pallas_call | solution.py:167
  (1 shorter events, 0.0 us)
Async XLA Ops:
  0.0 9.7 %collective-permute-start = (bf16[320,128]{1,0:T(8,128)(2,1)}, bf16[320,128]{1,0:T(8,128)(2,1)S(1)}, u32[]{:S(2)}, u32[]{:S(2)}) collective-permute-start(bf16[320,128]{1,0:T(8,128)(2,1)} %own_ref.1), channel_id=1, source_target_pairs={{2,4},{6,8},{10,12},{14,16},{18,20},{22,24},{26,28},{30,0},{4,2},{... | collective-permute-start | bytes 245768 | tf_op jit(solution)/shard_map/ppermute | solution.py:131
  6.9 4.7 %collective-permute-start.1 = (bf16[320,128]{1,0:T(8,128)(2,1)}, bf16[320,128]{1,0:T(8,128)(2,1)S(1)}, u32[]{:S(2)}, u32[]{:S(2)}) collective-permute-start(bf16[320,128]{1,0:T(8,128)(2,1)} %own_ref.1), channel_id=1, source_target_pairs={{0,2},{4,6},{8,10},{12,14},{16,18},{20,22},{24,26},{28,30},{2,0},{... | collective-permute-start | bytes 245768 | tf_op jit(solution)/shard_map/ppermute | solution.py:131
  6.9 2.2 %copy-start = (bf16[4,64,64,128]{3,2,1,0:T(8,128)(2,1)S(1)}, bf16[4,64,64,128]{3,2,1,0:T(8,128)(2,1)}, u32[]{:S(2)}) copy-start(bf16[4,64,64,128]{3,2,1,0:T(8,128)(2,1)} %source.1) | copy-start | bytes 12582916
  9.1 2.5 %copy-start.1 = (bf16[320,128]{1,0:T(8,128)(2,1)S(1)}, bf16[320,128]{1,0:T(8,128)(2,1)}, u32[]{:S(2)}) copy-start(bf16[320,128]{1,0:T(8,128)(2,1)} %own_ref.1) | copy-start | bytes 245764
  9.1 2.5 %copy-start.2 = (s32[4,2]{0,1:T(2,128)S(1)}, s32[4,2]{0,1:T(2,128)}, u32[]{:S(2)}) copy-start(s32[4,2]{0,1:T(2,128)} %param.7) | copy-start | bytes 100
  9.4 13.2 %copy-start.3 = (s32[112]{0:T(128)S(1)}, s32[112]{0:T(128)}, u32[]{:S(2)}) copy-start(s32[112]{0:T(128)} %param.8) | copy-start | bytes 1348
  14.7 1.4 %collective-permute-start.2 = (f32[4,4,16,128]{3,2,1,0:T(8,128)S(1)}, f32[4,4,16,128]{3,2,1,0:T(8,128)S(1)}, u32[]{:S(2)}, u32[]{:S(2)}) collective-permute-start(f32[4,4,16,128]{3,2,1,0:T(8,128)S(1)} %get-tuple-element.12), channel_id=1, source_target_pairs={{0,1},{1,0},{2,3},{3,2},{4,5},{5,4},{6,7},{7,6},{8,9},{9,8},{10,11... | collective-permute-start | bytes 393224 | tf_op jit(solution)/shard_map/ppermute | solution.py:127
  16.1 5.8 %collective-permute-start.3 = (f32[4,16,128]{2,1,0:T(8,128)S(1)}, f32[4,16,128]{2,1,0:T(8,128)S(1)}, u32[]{:S(2)}, u32[]{:S(2)}) collective-permute-start(f32[4,16,128]{2,1,0:T(8,128)S(1)} %get-tuple-element.14), channel_id=1, source_target_pairs={{0,8},{2,10},{4,12},{6,14},{8,16},{10,18},{12,20},{14,22},{16,24},... | collective-permute-start | bytes 98312 | tf_op jit(solution)/shard_map/ppermute | solution.py:127
  16.2 6.4 %collective-permute-start.4 = (f32[4,16,128]{2,1,0:T(8,128)S(1)}, f32[4,16,128]{2,1,0:T(8,128)S(1)}, u32[]{:S(2)}, u32[]{:S(2)}) collective-permute-start(f32[4,16,128]{2,1,0:T(8,128)S(1)} %get-tuple-element.15), channel_id=1, source_target_pairs={{0,16},{2,18},{4,20},{6,22},{8,24},{10,26},{12,28},{14,30},{16,0},... | collective-permute-start | bytes 98312 | tf_op jit(solution)/shard_map/ppermute | solution.py:127
  17.5 5.1 %collective-permute-start.5 = (f32[4,16,128]{2,1,0:T(8,128)S(1)}, f32[4,16,128]{2,1,0:T(8,128)S(1)}, u32[]{:S(2)}, u32[]{:S(2)}) collective-permute-start(f32[4,16,128]{2,1,0:T(8,128)S(1)} %get-tuple-element.16), channel_id=1, source_target_pairs={{0,30},{2,0},{4,2},{6,4},{8,6},{10,8},{12,10},{14,12},{16,14},{18,... | collective-permute-start | bytes 98312 | tf_op jit(solution)/shard_map/ppermute | solution.py:127

commit v3 on v2

--- a/solution.py
+++ b/solution.py
@@ -8,7 +8,14 @@
 from jax.sharding import PartitionSpec as P
 
 LANES = 128
-CHUNK = 16
+ROUTES = {
+    16: [
+        [8, 9, 10, 2, 12, 4, 5, 11, 7, 13, 14, 15, 0, 1, 6, 3],
+        [4, 5, 6, 7, 8, 13, 10, 15, 0, 1, 9, 3, 11, 12, 2, 14],
+        [15, 0, 1, 11, 3, 9, 14, 6, 12, 8, 2, 10, 4, 5, 13, 7],
+    ],
+}
+CHUNK = 8
 VMEM = pl.BlockSpec(memory_space=pltpu.VMEM)
 SMEM = pl.BlockSpec(memory_space=pltpu.SMEM)
 
@@ -19,7 +26,7 @@
     copy.wait()
 
 
-def build_kernel(groups, parts, blocks_ref, far_ref, own_ref, near_ref, three_ref, *rest):
+def build_kernel(groups, parts, blocks_ref, near_ref, own_ref, far_ref, three_ref, *rest):
     outs, (near, sel, half, acc, panels) = rest[:parts], rest[parts:]
     entries, aux_count, block, depth = three_ref.shape
     tiles = depth // block
@@ -30,7 +37,7 @@
 
     offset = lax.rem(blocks_ref[...] - (position - 1) * per_shard + groups * per_shard, groups * per_shard)
     side, within = lax.div(offset, per_shard), lax.rem(offset, per_shard)
-    offsets = (jnp.where(lax.rem(position, 2) == 0, side, 2 - side) * per_shard + within).astype(jnp.float32)
+    offsets = ((2 - side) * per_shard + within).astype(jnp.float32)
     tile_at = lax.broadcasted_iota(jnp.int32, offsets.shape, 0)
     entry_at = lax.broadcasted_iota(jnp.int32, offsets.shape, 1)
 
@@ -83,29 +90,58 @@
                 outs[r][j, k + 1] = jnp.where(low, pltpu.roll(even, block, 1), odd)
 
 
-def sum_kernel(parts, *refs):
+def route(groups, entries):
+    steps = [j * groups // entries for j in range(entries - 1)] + [groups - 1]
+    targets = ROUTES.get(groups) or [[(i + step) % groups for i in range(groups)] for step in steps[1:]]
+    sends = [[steps.index((t - i) % groups) for i, t in enumerate(each)] for each in targets]
+    takes = [[sent[each.index(i)] for i in range(groups)] for each, sent in zip(targets, sends)]
+    return targets, sends, takes
+
+
+def entry_of(table, position):
+    if len(set(table)) == 1:
+        return table[0]
+    packed = sum(value << (2 * i) for i, value in enumerate(table))
+    packed = jnp.int32(packed - (1 << 32) if packed >= 1 << 31 else packed)
+    return lax.shift_right_logical(packed, 2 * position) & 3
+
+
+def sum_kernel(parts, sends, *refs):
     terms, outs = refs[:parts], refs[parts:]
-    for j in range(len(outs)):
+    position = lax.axis_index("aux")
+    for out, table in zip(outs, [[0]] + sends):
+        j = entry_of(table, position)
         value = terms[0][j]
         for term in terms[1:]:
             value = value + term[j]
-        outs[j][...] = value
-
-
-def place_kernel(slot_ref, *refs):
+        out[...] = value
+
+
+def place_kernel(takes, slot_ref, *refs):
     terms, out_ref, rows = refs[:-2], refs[-2], refs[-1]
+    position = lax.axis_index("aux")
     entries, count = len(terms), terms[0].shape[1]
     band = 2 * entries - 1
+    given = [entry_of(table, position) for table in takes]
+
+    def term_of(j, k):
+        if j == 0:
+            return terms[0][k]
+        value = terms[1][k]
+        for o in range(1, len(given)):
+            value = jnp.where(given[o] == j, terms[1 + o][k], value)
+        return value
+
     for off in range(band):
         value = None
         for j in range(entries):
             k = off - (entries - 1) + j
             if 0 <= k < entries:
-                term = terms[j][k]
+                term = term_of(j, k)
                 value = term if value is None else value + term
         rows[pl.ds(off, count, stride=8), :] = value
     shape = (8, slot_ref.shape[1])
-    lines = lax.broadcasted_iota(jnp.int32, shape, 0) + lax.axis_index("aux") * band
+    lines = lax.broadcasted_iota(jnp.int32, shape, 0) + position * band
     offs = lax.rem(lax.broadcasted_iota(jnp.int32, shape, 1), band).astype(jnp.float32)
     order = jnp.sum(jnp.where(slot_ref[...] == lines, offs, 0.0), axis=1, keepdims=True).astype(jnp.int32)
     order = jnp.broadcast_to(jnp.minimum(order, 7), (8, LANES))
@@ -130,8 +166,8 @@
         pairs = [((i + first) % groups, (i + first + 1) % groups) for i in range(0, groups, 2)]
         return lax.ppermute(value, "aux", pairs + [(b, a) for a, b in pairs])
 
-    neighbour = swap(coefficients, 0)
-    other = swap(coefficients, 1)
+    other = shift(coefficients, "aux", -1)
+    neighbour = shift(coefficients, "aux", 1)
     held = pl.pallas_call(
         fetch_kernel,
         out_shape=jax.ShapeDtypeStruct(three_index.shape, three_index.dtype),
@@ -153,19 +189,21 @@
             pltpu.VMEM((entries // 2, entries * block, LANES), jnp.float32),
         ],
         compiler_params=pltpu.CompilerParams(vmem_limit_bytes=12 * 1024 * 1024),
-    )(basis_blocks.T, other, coefficients, neighbour, held)
+    )(basis_blocks.T, neighbour, coefficients, other, held)
     terms = [pieces[0]] + [shift(pieces[r], "occ", r) for r in range(1, parts)]
+    targets, sends, takes = route(groups, entries)
     rows = pl.pallas_call(
-        functools.partial(sum_kernel, parts),
+        functools.partial(sum_kernel, parts, sends),
         out_shape=[jax.ShapeDtypeStruct((entries, count, LANES), jnp.float32)] * entries,
         in_specs=[VMEM] * parts,
         out_specs=[VMEM] * entries,
         compiler_params=pltpu.CompilerParams(vmem_limit_bytes=4 * 1024 * 1024),
     )(*terms)
-    steps = [j * groups // entries for j in range(entries - 1)] + [groups - 1]
-    moved = [rows[0]] + [shift(rows[j], "aux", steps[j]) for j in range(1, entries)]
+    moved = [rows[0]]
+    for value, each in zip(rows[1:], targets):
+        moved.append(lax.ppermute(value, "aux", list(enumerate(each))))
     return pl.pallas_call(
-        place_kernel,
+        functools.partial(place_kernel, takes),
         out_shape=jax.ShapeDtypeStruct((band, count * LANES), jnp.float32),
         in_specs=[VMEM] * (entries + 1),
         out_specs=VMEM,

time: 23.6 us -> 22.4 us (0.949)
  waiting for transfers between devices: 6.14 us -> 3.18 us
  starting transfers between devices: 10.8 us -> 12.4 us
  local copies, waits for them, and re-layouts: 2.2 us -> 2.52 us
    ppermute x4 -> x3, starting transfers between devices: 3.9 us -> 7.01 us  [shift(): lax.ppermute(value, axis, [(i, (i + by) % size) for i in range(size)])]
    ppermute x4 -> x3, waiting for transfers between devices: 3.99 us -> 1.59 us  [shift(): lax.ppermute(value, axis, [(i, (i + by) % size) for i in range(size)])]
    ppermute x2 -> x3, starting transfers between devices: 6.93 us -> 5.36 us  [per_device(): moved.append(lax.ppermute(value, 'aux', list(enumerate(each))))]
    ppermute x2 -> x3, waiting for transfers between devices: 2.15 us -> 1.6 us  [per_device(): moved.append(lax.ppermute(value, 'aux', list(enumerate(each))))]
    unnamed x8, local copies, waits for them, and re-layouts: 2.2 us -> 2.52 us
where the time goes in v3:
time: 22.4 us; the launch traced here: 22.1 us
  starting transfers between devices  12.4 us (55%)
  Pallas kernels  4.01 us (18%)
  waiting for transfers between devices  3.18 us (14%)
  local copies, waits for them, and re-layouts  2.52 us (11%)
    ppermute x3, starting transfers between devices, shift(): lax.ppermute(value, axis, [(i, (i + by) % size) for i in range(size)])  7.01 us
    ppermute x3, starting transfers between devices, per_device(): moved.append(lax.ppermute(value, 'aux', list(enumerate(each))))  5.36 us
    pallas_call x1, Pallas kernels, per_device(): pl.pallas_call(functools.partial(build_kernel, groups, parts), out_shape=...  2.98 us
    unnamed x8, local copies, waits for them, and re-layouts  2.52 us
    ppermute x3, waiting for transfers between devices, per_device(): moved.append(lax.ppermute(value, 'aux', list(enumerate(each))))  1.6 us
    ppermute x3, waiting for transfers between devices, shift(): lax.ppermute(value, axis, [(i, (i + by) % size) for i in range(size)])  1.59 us
    pallas_call x1, Pallas kernels, per_device(): pl.pallas_call(functools.partial(place_kernel, takes), out_shape=jax.Shap...  0.73 us
  transfers between devices with their start and end apart: 6, of which 5 were waited for; matrix products, arithmetic and copies ran while one was open for 0% of the time, Pallas kernels for 1%

profile of v3, /device:TPU:0, one launch (start us, length us, event | category | flops | bytes accessed | tf_op | source)
XLA Modules:
  0.0 22.1 jit_solution(14956507826869356897)
XLA Ops:
  0.0 2.9 %collective-permute-start = (bf16[320,128]{1,0:T(8,128)(2,1)}, bf16[320,128]{1,0:T(8,128)(2,1)S(1)}, u32[]{:S(2)}, u32[]{:S(2)}) collective-permute-start(bf16[320,128]{1,0:T(8,128)(2,1)} %own_ref.1), channel_id=1, source_target_pairs={{0,2},{2,4},{4,6},{6,8},{8,10},{10,12},{12,14},{14,16},{16,18},{18... | collective-permute-start | bytes 245768 | tf_op jit(solution)/shard_map/ppermute | solution.py:163
  2.9 4.0 %collective-permute-start.1 = (bf16[320,128]{1,0:T(8,128)(2,1)}, bf16[320,128]{1,0:T(8,128)(2,1)S(1)}, u32[]{:S(2)}, u32[]{:S(2)}) collective-permute-start(bf16[320,128]{1,0:T(8,128)(2,1)} %own_ref.1), channel_id=1, source_target_pairs={{0,30},{2,0},{4,2},{6,4},{8,6},{10,8},{12,10},{14,12},{16,14},{18,... | collective-permute-start | bytes 245768 | tf_op jit(solution)/shard_map/ppermute | solution.py:163
  6.9 0.0 copy-start
  6.9 2.2 %copy-done = bf16[4,64,64,128]{3,2,1,0:T(8,128)(2,1)S(1)} copy-done((bf16[4,64,64,128]{3,2,1,0:T(8,128)(2,1)S(1)}, bf16[4,64,64,128]{3,2,1,0:T(8,128)(2,1)}, u32[]{:S(2)}) %copy-start) | copy-done | bytes 4194328
  9.1 0.0 copy-start.1
  9.1 0.0 copy-start.2
  9.1 0.3 %shard_map.46.three_ref = bf16[4,64,64,128]{3,2,1,0:T(8,128)(2,1)S(1)} custom-call(bf16[4,64,64,128]{3,2,1,0:T(8,128)(2,1)S(1)} %copy-done), custom_call_target="tpu_custom_call" | custom-call | tf_op jit(solution)/shard_map/pallas_call | solution.py:171
  9.4 0.0 copy-start.3
  9.4 0.2 %collective-permute-done.near_ref = bf16[320,128]{1,0:T(8,128)(2,1)S(1)} collective-permute-done((bf16[320,128]{1,0:T(8,128)(2,1)}, bf16[320,128]{1,0:T(8,128)(2,1)S(1)}, u32[]{:S(2)}, u32[]{:S(2)}) %collective-permute-start) | collective-permute-done | bytes 81952 | tf_op jit(solution)/shard_map/ppermute | solution.py:163
  9.7 0.0 collective-permute-done.1.far_ref
  9.7 0.3 %copy-done.1 = bf16[320,128]{1,0:T(8,128)(2,1)S(1)} copy-done((bf16[320,128]{1,0:T(8,128)(2,1)S(1)}, bf16[320,128]{1,0:T(8,128)(2,1)}, u32[]{:S(2)}) %copy-start.1) | copy-done | bytes 81944
  10.0 0.0 copy-done.2
  10.0 3.0 %shard_map.47 = (f32[4,4,16,128]{3,2,1,0:T(8,128)S(1)}, f32[4,4,16,128]{3,2,1,0:T(8,128)S(1)}) custom-call(s32[2,4]{1,0:T(2,128)S(1)} %bitcast.2, bf16[320,128]{1,0:T(8,128)(2,1)S(1)} %collective-permute-done.near_ref, bf16[320,128]{1,0:T(8,128)(2,1)S(1)} %copy-done.1, bf16[320,128]{1,0:T(8,128)(2,1)S(1)} %collective-permute-done.1.far_ref, ...), custom_call_target="tpu_custom_call" | custom-call | tf_op jit(solution)/shard_map/pallas_call | solution.py:179
  13.0 0.1 collective-permute-start.2
  13.1 1.3 %collective-permute-done.2.refs_1_ = f32[4,4,16,128]{3,2,1,0:T(8,128)S(1)} collective-permute-done((f32[4,4,16,128]{3,2,1,0:T(8,128)S(1)}, f32[4,4,16,128]{3,2,1,0:T(8,128)S(1)}, u32[]{:S(2)}, u32[]{:S(2)}) %collective-permute-start.2) | collective-permute-done | bytes 131104 | tf_op jit(solution)/shard_map/ppermute | solution.py:163
  14.4 1.2 %collective-permute-start.3 = (f32[4,16,128]{2,1,0:T(8,128)S(1)}, f32[4,16,128]{2,1,0:T(8,128)S(1)}, u32[]{:S(2)}, u32[]{:S(2)}) collective-permute-start(f32[4,16,128]{2,1,0:T(8,128)S(1)} %get-tuple-element.14), channel_id=1, source_target_pairs={{0,16},{2,18},{4,20},{6,4},{8,24},{10,8},{12,10},{14,22},{16,14},{... | collective-permute-start | bytes 98312 | tf_op jit(solution)/shard_map/ppermute | solution.py:204
  15.6 1.6 %collective-permute-start.4 = (f32[4,16,128]{2,1,0:T(8,128)S(1)}, f32[4,16,128]{2,1,0:T(8,128)S(1)}, u32[]{:S(2)}, u32[]{:S(2)}) collective-permute-start(f32[4,16,128]{2,1,0:T(8,128)S(1)} %get-tuple-element.15), channel_id=1, source_target_pairs={{0,8},{2,10},{4,12},{6,14},{8,16},{10,26},{12,20},{14,30},{16,0},{... | collective-permute-start | bytes 98312 | tf_op jit(solution)/shard_map/ppermute | solution.py:204
  17.2 2.6 %collective-permute-start.5 = (f32[4,16,128]{2,1,0:T(8,128)S(1)}, f32[4,16,128]{2,1,0:T(8,128)S(1)}, u32[]{:S(2)}, u32[]{:S(2)}) collective-permute-start(f32[4,16,128]{2,1,0:T(8,128)S(1)} %get-tuple-element.16), channel_id=1, source_target_pairs={{0,30},{2,0},{4,2},{6,22},{8,6},{10,18},{12,28},{14,12},{16,24},{1... | collective-permute-start | bytes 98312 | tf_op jit(solution)/shard_map/ppermute | solution.py:204
  19.8 0.5 %collective-permute-done.3.refs_1_ = f32[4,16,128]{2,1,0:T(8,128)S(1)} collective-permute-done((f32[4,16,128]{2,1,0:T(8,128)S(1)}, f32[4,16,128]{2,1,0:T(8,128)S(1)}, u32[]{:S(2)}, u32[]{:S(2)}) %collective-permute-start.3) | collective-permute-done | bytes 32800 | tf_op jit(solution)/shard_map/ppermute | solution.py:204
  20.3 1.0 %collective-permute-done.4.refs_2_ = f32[4,16,128]{2,1,0:T(8,128)S(1)} collective-permute-done((f32[4,16,128]{2,1,0:T(8,128)S(1)}, f32[4,16,128]{2,1,0:T(8,128)S(1)}, u32[]{:S(2)}, u32[]{:S(2)}) %collective-permute-start.4) | collective-permute-done | bytes 32800 | tf_op jit(solution)/shard_map/ppermute | solution.py:204
  21.3 0.1 collective-permute-done.5.refs_3_
  21.4 0.0 copy-done.3
  21.4 0.7 %shard_map.49 = f32[7,2048]{1,0:T(8,128)} custom-call(s32[1,112]{1,0:T(1,128)S(1)} %bitcast.3, f32[4,16,128]{2,1,0:T(8,128)S(1)} %get-tuple-element.13.refs_0_, f32[4,16,128]{2,1,0:T(8,128)S(1)} %collective-permute-done.3.refs_1_, f32[4,16,128]{2,1,0:T(8,128)S(1)} %collective-permute-done.4.refs_2_, f32[4,16,128]{2,1,0:T(8,128)S(1)} %collective-permute-done.5.refs_3_), custom_call_target="tpu_custom_call" | custom-call | tf_op jit(solution)/shard_map/pallas_call | solution.py:205
  (1 shorter events, 0.0 us)
Async XLA Ops:
  0.0 9.7 %collective-permute-start = (bf16[320,128]{1,0:T(8,128)(2,1)}, bf16[320,128]{1,0:T(8,128)(2,1)S(1)}, u32[]{:S(2)}, u32[]{:S(2)}) collective-permute-start(bf16[320,128]{1,0:T(8,128)(2,1)} %own_ref.1), channel_id=1, source_target_pairs={{0,2},{2,4},{4,6},{6,8},{8,10},{10,12},{12,14},{14,16},{16,18},{18... | collective-permute-start | bytes 245768 | tf_op jit(solution)/shard_map/ppermute | solution.py:163
  2.9 6.8 %collective-permute-start.1 = (bf16[320,128]{1,0:T(8,128)(2,1)}, bf16[320,128]{1,0:T(8,128)(2,1)S(1)}, u32[]{:S(2)}, u32[]{:S(2)}) collective-permute-start(bf16[320,128]{1,0:T(8,128)(2,1)} %own_ref.1), channel_id=1, source_target_pairs={{0,30},{2,0},{4,2},{6,4},{8,6},{10,8},{12,10},{14,12},{16,14},{18,... | collective-permute-start | bytes 245768 | tf_op jit(solution)/shard_map/ppermute | solution.py:163
  6.9 2.2 %copy-start = (bf16[4,64,64,128]{3,2,1,0:T(8,128)(2,1)S(1)}, bf16[4,64,64,128]{3,2,1,0:T(8,128)(2,1)}, u32[]{:S(2)}) copy-start(bf16[4,64,64,128]{3,2,1,0:T(8,128)(2,1)} %source.1) | copy-start | bytes 12582916
  9.1 0.9 %copy-start.1 = (bf16[320,128]{1,0:T(8,128)(2,1)S(1)}, bf16[320,128]{1,0:T(8,128)(2,1)}, u32[]{:S(2)}) copy-start(bf16[320,128]{1,0:T(8,128)(2,1)} %own_ref.1) | copy-start | bytes 245764
  9.1 0.9 %copy-start.2 = (s32[4,2]{0,1:T(2,128)S(1)}, s32[4,2]{0,1:T(2,128)}, u32[]{:S(2)}) copy-start(s32[4,2]{0,1:T(2,128)} %param.7) | copy-start | bytes 100
  9.4 12.0 %copy-start.3 = (s32[112]{0:T(128)S(1)}, s32[112]{0:T(128)}, u32[]{:S(2)}) copy-start(s32[112]{0:T(128)} %param.8) | copy-start | bytes 1348
  13.0 1.4 %collective-permute-start.2 = (f32[4,4,16,128]{3,2,1,0:T(8,128)S(1)}, f32[4,4,16,128]{3,2,1,0:T(8,128)S(1)}, u32[]{:S(2)}, u32[]{:S(2)}) collective-permute-start(f32[4,4,16,128]{3,2,1,0:T(8,128)S(1)} %get-tuple-element.12), channel_id=1, source_target_pairs={{0,1},{1,0},{2,3},{3,2},{4,5},{5,4},{6,7},{7,6},{8,9},{9,8},{10,11... | collective-permute-start | bytes 393224 | tf_op jit(solution)/shard_map/ppermute | solution.py:163
  14.4 5.9 %collective-permute-start.3 = (f32[4,16,128]{2,1,0:T(8,128)S(1)}, f32[4,16,128]{2,1,0:T(8,128)S(1)}, u32[]{:S(2)}, u32[]{:S(2)}) collective-permute-start(f32[4,16,128]{2,1,0:T(8,128)S(1)} %get-tuple-element.14), channel_id=1, source_target_pairs={{0,16},{2,18},{4,20},{6,4},{8,24},{10,8},{12,10},{14,22},{16,14},{... | collective-permute-start | bytes 98312 | tf_op jit(solution)/shard_map/ppermute | solution.py:204
  15.6 5.7 %collective-permute-start.4 = (f32[4,16,128]{2,1,0:T(8,128)S(1)}, f32[4,16,128]{2,1,0:T(8,128)S(1)}, u32[]{:S(2)}, u32[]{:S(2)}) collective-permute-start(f32[4,16,128]{2,1,0:T(8,128)S(1)} %get-tuple-element.15), channel_id=1, source_target_pairs={{0,8},{2,10},{4,12},{6,14},{8,16},{10,26},{12,20},{14,30},{16,0},{... | collective-permute-start | bytes 98312 | tf_op jit(solution)/shard_map/ppermute | solution.py:204
  17.2 4.2 %collective-permute-start.5 = (f32[4,16,128]{2,1,0:T(8,128)S(1)}, f32[4,16,128]{2,1,0:T(8,128)S(1)}, u32[]{:S(2)}, u32[]{:S(2)}) collective-permute-start(f32[4,16,128]{2,1,0:T(8,128)S(1)} %get-tuple-element.16), channel_id=1, source_target_pairs={{0,30},{2,0},{4,2},{6,22},{8,6},{10,18},{12,28},{14,12},{16,24},{1... | collective-permute-start | bytes 98312 | tf_op jit(solution)/shard_map/ppermute | solution.py:204

commit v4 on v3

--- a/solution.py
+++ b/solution.py
@@ -20,10 +20,12 @@
 SMEM = pl.BlockSpec(memory_space=pltpu.SMEM)
 
 
-def fetch_kernel(source, target, sem):
-    copy = pltpu.make_async_copy(source, target, sem)
-    copy.start()
-    copy.wait()
+def fetch_kernel(source, target, sems):
+    copies = [pltpu.make_async_copy(source.at[e], target.at[e], sems.at[e]) for e in range(source.shape[0])]
+    for copy in copies:
+        copy.start()
+    for copy in copies:
+        copy.wait()
 
 
 def build_kernel(groups, parts, blocks_ref, near_ref, own_ref, far_ref, three_ref, *rest):
@@ -173,8 +175,8 @@
         out_shape=jax.ShapeDtypeStruct(three_index.shape, three_index.dtype),
         in_specs=[pl.BlockSpec(memory_space=pl.ANY)],
         out_specs=VMEM,
-        scratch_shapes=[pltpu.SemaphoreType.DMA],
-        compiler_params=pltpu.CompilerParams(vmem_limit_bytes=8 * 1024 * 1024),
+        scratch_shapes=[pltpu.SemaphoreType.DMA((entries,))],
+        compiler_params=pltpu.CompilerParams(vmem_limit_bytes=47 * 1024 * 1024),
     )(three_index)
     pieces = pl.pallas_call(
         functools.partial(build_kernel, groups, parts),

time: 22.4 us -> 22.4 us (level)
  local copies, waits for them, and re-layouts: 2.52 us -> 0.01 us
  Pallas kernels: 4.01 us -> 5.94 us
  starting transfers between devices: 12.4 us -> 12.7 us
  waiting for transfers between devices: 3.18 us -> 3.47 us
    unnamed x8 -> x6, local copies, waits for them, and re-layouts: 2.52 us -> 0.01 us
    pallas_call x1, Pallas kernels: 0.29 us -> 2.2 us  [per_device(): pl.pallas_call(fetch_kernel, out_shape=jax.ShapeDtypeStruct(three_index.s...]
    ppermute x3, starting transfers between devices: 5.36 us -> 5.65 us  [per_device(): moved.append(lax.ppermute(value, 'aux', list(enumerate(each))))]
    ppermute x3, waiting for transfers between devices: 1.59 us -> 1.88 us  [shift(): lax.ppermute(value, axis, [(i, (i + by) % size) for i in range(size)])]
  transfers between devices with their start and end apart: 6 -> 6, of which waited for: 5 -> 5; matrix products, arithmetic and copies ran while one was open for 0% -> 0% of each run, Pallas kernels for 1% -> 10%
where the time goes in v4:
time: 22.4 us; the launch traced here: 22.2 us
  starting transfers between devices  12.7 us (57%)
  Pallas kernels  5.94 us (27%)
  waiting for transfers between devices  3.47 us (15%)
    ppermute x3, starting transfers between devices, shift(): lax.ppermute(value, axis, [(i, (i + by) % size) for i in range(size)])  7.06 us
    ppermute x3, starting transfers between devices, per_device(): moved.append(lax.ppermute(value, 'aux', list(enumerate(each))))  5.65 us
    pallas_call x1, Pallas kernels, per_device(): pl.pallas_call(functools.partial(build_kernel, groups, parts), out_shape=...  2.99 us
    pallas_call x1, Pallas kernels, per_device(): pl.pallas_call(fetch_kernel, out_shape=jax.ShapeDtypeStruct(three_index.s...  2.2 us
    ppermute x3, waiting for transfers between devices, shift(): lax.ppermute(value, axis, [(i, (i + by) % size) for i in range(size)])  1.88 us
    ppermute x3, waiting for transfers between devices, per_device(): moved.append(lax.ppermute(value, 'aux', list(enumerate(each))))  1.6 us
    pallas_call x1, Pallas kernels, per_device(): pl.pallas_call(functools.partial(place_kernel, takes), out_shape=jax.Shap...  0.73 us
  transfers between devices with their start and end apart: 6, of which 5 were waited for; matrix products, arithmetic and copies ran while one was open for 0% of the time, Pallas kernels for 10%

profile of v4, /device:TPU:0, one launch (start us, length us, event | category | flops | bytes accessed | tf_op | source)
XLA Modules:
  0.0 22.2 jit_solution(1252645415894518993)
XLA Ops:
  0.0 0.0 copy-start
  0.0 0.0 copy-start.1
  0.0 2.9 %collective-permute-start = (bf16[320,128]{1,0:T(8,128)(2,1)}, bf16[320,128]{1,0:T(8,128)(2,1)S(1)}, u32[]{:S(2)}, u32[]{:S(2)}) collective-permute-start(bf16[320,128]{1,0:T(8,128)(2,1)} %own_ref.1), channel_id=1, source_target_pairs={{0,2},{2,4},{4,6},{6,8},{8,10},{10,12},{12,14},{14,16},{16,18},{18... | collective-permute-start | bytes 245768 | tf_op jit(solution)/shard_map/ppermute | solution.py:165
  2.9 4.1 %collective-permute-start.1 = (bf16[320,128]{1,0:T(8,128)(2,1)}, bf16[320,128]{1,0:T(8,128)(2,1)S(1)}, u32[]{:S(2)}, u32[]{:S(2)}) collective-permute-start(bf16[320,128]{1,0:T(8,128)(2,1)} %own_ref.1), channel_id=1, source_target_pairs={{0,30},{2,0},{4,2},{6,4},{8,6},{10,8},{12,10},{14,12},{16,14},{18,... | collective-permute-start | bytes 245768 | tf_op jit(solution)/shard_map/ppermute | solution.py:165
  7.0 2.2 %shard_map.46.three_ref = bf16[4,64,64,128]{3,2,1,0:T(8,128)(2,1)S(1)} custom-call(bf16[4,64,64,128]{3,2,1,0:T(8,128)(2,1)} %source.1), custom_call_target="tpu_custom_call" | custom-call | tf_op jit(solution)/shard_map/pallas_call | solution.py:173
  9.2 0.0 copy-start.2
  9.2 0.5 %collective-permute-done.near_ref = bf16[320,128]{1,0:T(8,128)(2,1)S(1)} collective-permute-done((bf16[320,128]{1,0:T(8,128)(2,1)}, bf16[320,128]{1,0:T(8,128)(2,1)S(1)}, u32[]{:S(2)}, u32[]{:S(2)}) %collective-permute-start) | collective-permute-done | bytes 81952 | tf_op jit(solution)/shard_map/ppermute | solution.py:165
  9.8 0.0 collective-permute-done.1.far_ref
  9.8 0.0 copy-done
  9.8 0.0 copy-done.1
  9.8 3.0 %shard_map.47 = (f32[4,4,16,128]{3,2,1,0:T(8,128)S(1)}, f32[4,4,16,128]{3,2,1,0:T(8,128)S(1)}) custom-call(s32[2,4]{1,0:T(2,128)S(1)} %bitcast.2, bf16[320,128]{1,0:T(8,128)(2,1)S(1)} %collective-permute-done.near_ref, bf16[320,128]{1,0:T(8,128)(2,1)S(1)} %copy-done, bf16[320,128]{1,0:T(8,128)(2,1)S(1)} %collective-permute-done.1.far_ref, ...), custom_call_target="tpu_custom_call" | custom-call | tf_op jit(solution)/shard_map/pallas_call | solution.py:181
  12.8 0.1 collective-permute-start.2
  12.8 1.3 %collective-permute-done.2.refs_1_ = f32[4,4,16,128]{3,2,1,0:T(8,128)S(1)} collective-permute-done((f32[4,4,16,128]{3,2,1,0:T(8,128)S(1)}, f32[4,4,16,128]{3,2,1,0:T(8,128)S(1)}, u32[]{:S(2)}, u32[]{:S(2)}) %collective-permute-start.2) | collective-permute-done | bytes 131104 | tf_op jit(solution)/shard_map/ppermute | solution.py:165
  14.2 1.4 %collective-permute-start.3 = (f32[4,16,128]{2,1,0:T(8,128)S(1)}, f32[4,16,128]{2,1,0:T(8,128)S(1)}, u32[]{:S(2)}, u32[]{:S(2)}) collective-permute-start(f32[4,16,128]{2,1,0:T(8,128)S(1)} %get-tuple-element.14), channel_id=1, source_target_pairs={{0,16},{2,18},{4,20},{6,4},{8,24},{10,8},{12,10},{14,22},{16,14},{... | collective-permute-start | bytes 98312 | tf_op jit(solution)/shard_map/ppermute | solution.py:206
  15.6 1.6 %collective-permute-start.4 = (f32[4,16,128]{2,1,0:T(8,128)S(1)}, f32[4,16,128]{2,1,0:T(8,128)S(1)}, u32[]{:S(2)}, u32[]{:S(2)}) collective-permute-start(f32[4,16,128]{2,1,0:T(8,128)S(1)} %get-tuple-element.15), channel_id=1, source_target_pairs={{0,8},{2,10},{4,12},{6,14},{8,16},{10,26},{12,20},{14,30},{16,0},{... | collective-permute-start | bytes 98312 | tf_op jit(solution)/shard_map/ppermute | solution.py:206
  17.2 2.7 %collective-permute-start.5 = (f32[4,16,128]{2,1,0:T(8,128)S(1)}, f32[4,16,128]{2,1,0:T(8,128)S(1)}, u32[]{:S(2)}, u32[]{:S(2)}) collective-permute-start(f32[4,16,128]{2,1,0:T(8,128)S(1)} %get-tuple-element.16), channel_id=1, source_target_pairs={{0,30},{2,0},{4,2},{6,22},{8,6},{10,18},{12,28},{14,12},{16,24},{1... | collective-permute-start | bytes 98312 | tf_op jit(solution)/shard_map/ppermute | solution.py:206
  19.9 0.2 collective-permute-done.3.refs_1_
  20.1 1.2 %collective-permute-done.4.refs_2_ = f32[4,16,128]{2,1,0:T(8,128)S(1)} collective-permute-done((f32[4,16,128]{2,1,0:T(8,128)S(1)}, f32[4,16,128]{2,1,0:T(8,128)S(1)}, u32[]{:S(2)}, u32[]{:S(2)}) %collective-permute-start.4) | collective-permute-done | bytes 32800 | tf_op jit(solution)/shard_map/ppermute | solution.py:206
  21.3 0.2 collective-permute-done.5.refs_3_
  21.5 0.0 copy-done.2
  21.5 0.7 %shard_map.49 = f32[7,2048]{1,0:T(8,128)} custom-call(s32[1,112]{1,0:T(1,128)S(1)} %bitcast.3, f32[4,16,128]{2,1,0:T(8,128)S(1)} %get-tuple-element.13.refs_0_, f32[4,16,128]{2,1,0:T(8,128)S(1)} %collective-permute-done.3.refs_1_, f32[4,16,128]{2,1,0:T(8,128)S(1)} %collective-permute-done.4.refs_2_, f32[4,16,128]{2,1,0:T(8,128)S(1)} %collective-permute-done.5.refs_3_), custom_call_target="tpu_custom_call" | custom-call | tf_op jit(solution)/shard_map/pallas_call | solution.py:207
  (1 shorter events, 0.0 us)
Async XLA Ops:
  0.0 9.8 %copy-start = (bf16[320,128]{1,0:T(8,128)(2,1)S(1)}, bf16[320,128]{1,0:T(8,128)(2,1)}, u32[]{:S(2)}) copy-start(bf16[320,128]{1,0:T(8,128)(2,1)} %own_ref.1) | copy-start | bytes 245764
  0.0 9.8 %copy-start.1 = (s32[4,2]{0,1:T(2,128)S(1)}, s32[4,2]{0,1:T(2,128)}, u32[]{:S(2)}) copy-start(s32[4,2]{0,1:T(2,128)} %param.7) | copy-start | bytes 100
  0.0 9.8 %collective-permute-start = (bf16[320,128]{1,0:T(8,128)(2,1)}, bf16[320,128]{1,0:T(8,128)(2,1)S(1)}, u32[]{:S(2)}, u32[]{:S(2)}) collective-permute-start(bf16[320,128]{1,0:T(8,128)(2,1)} %own_ref.1), channel_id=1, source_target_pairs={{0,2},{2,4},{4,6},{6,8},{8,10},{10,12},{12,14},{14,16},{16,18},{18... | collective-permute-start | bytes 245768 | tf_op jit(solution)/shard_map/ppermute | solution.py:165
  2.9 6.8 %collective-permute-start.1 = (bf16[320,128]{1,0:T(8,128)(2,1)}, bf16[320,128]{1,0:T(8,128)(2,1)S(1)}, u32[]{:S(2)}, u32[]{:S(2)}) collective-permute-start(bf16[320,128]{1,0:T(8,128)(2,1)} %own_ref.1), channel_id=1, source_target_pairs={{0,30},{2,0},{4,2},{6,4},{8,6},{10,8},{12,10},{14,12},{16,14},{18,... | collective-permute-start | bytes 245768 | tf_op jit(solution)/shard_map/ppermute | solution.py:165
  9.2 12.2 %copy-start.2 = (s32[112]{0:T(128)S(1)}, s32[112]{0:T(128)}, u32[]{:S(2)}) copy-start(s32[112]{0:T(128)} %param.8) | copy-start | bytes 1348
  12.8 1.4 %collective-permute-start.2 = (f32[4,4,16,128]{3,2,1,0:T(8,128)S(1)}, f32[4,4,16,128]{3,2,1,0:T(8,128)S(1)}, u32[]{:S(2)}, u32[]{:S(2)}) collective-permute-start(f32[4,4,16,128]{3,2,1,0:T(8,128)S(1)} %get-tuple-element.12), channel_id=1, source_target_pairs={{0,1},{1,0},{2,3},{3,2},{4,5},{5,4},{6,7},{7,6},{8,9},{9,8},{10,11... | collective-permute-start | bytes 393224 | tf_op jit(solution)/shard_map/ppermute | solution.py:165
  14.2 5.9 %collective-permute-start.3 = (f32[4,16,128]{2,1,0:T(8,128)S(1)}, f32[4,16,128]{2,1,0:T(8,128)S(1)}, u32[]{:S(2)}, u32[]{:S(2)}) collective-permute-start(f32[4,16,128]{2,1,0:T(8,128)S(1)} %get-tuple-element.14), channel_id=1, source_target_pairs={{0,16},{2,18},{4,20},{6,4},{8,24},{10,8},{12,10},{14,22},{16,14},{... | collective-permute-start | bytes 98312 | tf_op jit(solution)/shard_map/ppermute | solution.py:206
  15.6 5.7 %collective-permute-start.4 = (f32[4,16,128]{2,1,0:T(8,128)S(1)}, f32[4,16,128]{2,1,0:T(8,128)S(1)}, u32[]{:S(2)}, u32[]{:S(2)}) collective-permute-start(f32[4,16,128]{2,1,0:T(8,128)S(1)} %get-tuple-element.15), channel_id=1, source_target_pairs={{0,8},{2,10},{4,12},{6,14},{8,16},{10,26},{12,20},{14,30},{16,0},{... | collective-permute-start | bytes 98312 | tf_op jit(solution)/shard_map/ppermute | solution.py:206
  17.2 4.3 %collective-permute-start.5 = (f32[4,16,128]{2,1,0:T(8,128)S(1)}, f32[4,16,128]{2,1,0:T(8,128)S(1)}, u32[]{:S(2)}, u32[]{:S(2)}) collective-permute-start(f32[4,16,128]{2,1,0:T(8,128)S(1)} %get-tuple-element.16), channel_id=1, source_target_pairs={{0,30},{2,0},{4,2},{6,22},{8,6},{10,18},{12,28},{14,12},{16,24},{1... | collective-permute-start | bytes 98312 | tf_op jit(solution)/shard_map/ppermute | solution.py:206

commit v5 on v4

--- a/solution.py
+++ b/solution.py
@@ -29,7 +29,7 @@
 
 
 def build_kernel(groups, parts, blocks_ref, near_ref, own_ref, far_ref, three_ref, *rest):
-    outs, (near, sel, half, acc, panels) = rest[:parts], rest[parts:]
+    outs, firsts, (near, sel, half, acc, panels) = rest[:parts], rest[parts : 2 * parts], rest[2 * parts :]
     entries, aux_count, block, depth = three_ref.shape
     tiles = depth // block
     shard_rows, orbitals = own_ref.shape
@@ -88,8 +88,9 @@
             for k in range(0, entries, 2):
                 even = panels[k // 2, pl.ds(base, count, stride=2), :]
                 odd = panels[k // 2, pl.ds(base + 1, count, stride=2), :]
-                outs[r][j, k] = jnp.where(low, even, pltpu.roll(odd, block, 1))
-                outs[r][j, k + 1] = jnp.where(low, pltpu.roll(even, block, 1), odd)
+                out = firsts[r] if j == 0 else outs[r].at[j - 1]
+                out[k] = jnp.where(low, even, pltpu.roll(odd, block, 1))
+                out[k + 1] = jnp.where(low, pltpu.roll(even, block, 1), odd)
 
 
 def route(groups, entries):
@@ -111,27 +112,27 @@
 def sum_kernel(parts, sends, *refs):
     terms, outs = refs[:parts], refs[parts:]
     position = lax.axis_index("aux")
-    for out, table in zip(outs, [[0]] + sends):
+    for out, table in zip(outs, sends):
         j = entry_of(table, position)
-        value = terms[0][j]
+        value = terms[0][j - 1]
         for term in terms[1:]:
-            value = value + term[j]
+            value = value + term[j - 1]
         out[...] = value
 
 
-def place_kernel(takes, slot_ref, *refs):
-    terms, out_ref, rows = refs[:-2], refs[-2], refs[-1]
+def place_kernel(parts, takes, slot_ref, *refs):
+    firsts, terms, out_ref, rows = refs[:parts], refs[parts:-2], refs[-2], refs[-1]
     position = lax.axis_index("aux")
-    entries, count = len(terms), terms[0].shape[1]
+    entries, count = firsts[0].shape[:2]
     band = 2 * entries - 1
     given = [entry_of(table, position) for table in takes]
 
     def term_of(j, k):
         if j == 0:
-            return terms[0][k]
-        value = terms[1][k]
+            return sum((first[k] for first in firsts[1:]), firsts[0][k])
+        value = terms[0][k]
         for o in range(1, len(given)):
-            value = jnp.where(given[o] == j, terms[1 + o][k], value)
+            value = jnp.where(given[o] == j, terms[o][k], value)
         return value
 
     for off in range(band):
@@ -180,9 +181,10 @@
     )(three_index)
     pieces = pl.pallas_call(
         functools.partial(build_kernel, groups, parts),
-        out_shape=[jax.ShapeDtypeStruct((entries, entries, count, LANES), jnp.float32)] * parts,
+        out_shape=[jax.ShapeDtypeStruct((entries - 1, entries, count, LANES), jnp.float32)] * parts
+        + [jax.ShapeDtypeStruct((entries, count, LANES), jnp.float32)] * parts,
         in_specs=[VMEM] * 5,
-        out_specs=[VMEM] * parts,
+        out_specs=[VMEM] * (2 * parts),
         scratch_shapes=[
             pltpu.VMEM((3 * shard_rows, orbitals), jnp.bfloat16),
             pltpu.VMEM((entries // 2, 2 * depth, 2 * orbitals), jnp.bfloat16),
@@ -196,22 +198,23 @@
     targets, sends, takes = route(groups, entries)
     rows = pl.pallas_call(
         functools.partial(sum_kernel, parts, sends),
-        out_shape=[jax.ShapeDtypeStruct((entries, count, LANES), jnp.float32)] * entries,
+        out_shape=[jax.ShapeDtypeStruct((entries, count, LANES), jnp.float32)] * (entries - 1),
         in_specs=[VMEM] * parts,
-        out_specs=[VMEM] * entries,
+        out_specs=[VMEM] * (entries - 1),
         compiler_params=pltpu.CompilerParams(vmem_limit_bytes=4 * 1024 * 1024),
     )(*terms)
-    moved = [rows[0]]
-    for value, each in zip(rows[1:], targets):
+    moved = []
+    for value, each in zip(rows, targets):
         moved.append(lax.ppermute(value, "aux", list(enumerate(each))))
+    firsts = [pieces[parts]] + [shift(pieces[parts + r], "occ", r) for r in range(1, parts)]
     return pl.pallas_call(
-        functools.partial(place_kernel, takes),
+        functools.partial(place_kernel, parts, takes),
         out_shape=jax.ShapeDtypeStruct((band, count * LANES), jnp.float32),
-        in_specs=[VMEM] * (entries + 1),
+        in_specs=[VMEM] * (entries + parts),
         out_specs=VMEM,
         scratch_shapes=[pltpu.VMEM((count * 8, LANES), jnp.float32)],
         compiler_params=pltpu.CompilerParams(vmem_limit_bytes=4 * 1024 * 1024),
-    )(fock_slot.reshape(1, -1), *moved)
+    )(fock_slot.reshape(1, -1), *firsts, *moved)
 
 
 def solution(mesh):

time: 22.4 us -> 22.4 us (level)
  waiting for transfers between devices: 3.47 us -> 2.93 us
  starting transfers between devices: 12.7 us -> 13.2 us
    ppermute x3 -> x4, waiting for transfers between devices: 1.88 us -> 1.34 us  [shift(): lax.ppermute(value, axis, [(i, (i + by) % size) for i in range(size)])]
    ppermute x3 -> x4, starting transfers between devices: 7.06 us -> 7.56 us  [shift(): lax.ppermute(value, axis, [(i, (i + by) % size) for i in range(size)])]
  transfers between devices with their start and end apart: 6 -> 7, of which waited for: 5 -> 5; matrix products, arithmetic and copies ran while one was open for 0% -> 0% of each run, Pallas kernels for 10% -> 10%
where the time goes in v5:
time: 22.4 us; the launch traced here: 22.1 us
  starting transfers between devices  13.2 us (59%)
  Pallas kernels  5.93 us (26%)
  waiting for transfers between devices  2.93 us (13%)
    ppermute x4, starting transfers between devices, shift(): lax.ppermute(value, axis, [(i, (i + by) % size) for i in range(size)])  7.56 us
    ppermute x3, starting transfers between devices, per_device(): moved.append(lax.ppermute(value, 'aux', list(enumerate(each))))  5.65 us
    pallas_call x1, Pallas kernels, per_device(): pl.pallas_call(functools.partial(build_kernel, groups, parts), out_shape=...  2.99 us
    pallas_call x1, Pallas kernels, per_device(): pl.pallas_call(fetch_kernel, out_shape=jax.ShapeDtypeStruct(three_index.s...  2.2 us
    ppermute x3, waiting for transfers between devices, per_device(): moved.append(lax.ppermute(value, 'aux', list(enumerate(each))))  1.59 us
    ppermute x4, waiting for transfers between devices, shift(): lax.ppermute(value, axis, [(i, (i + by) % size) for i in range(size)])  1.34 us
    pallas_call x1, Pallas kernels, per_device(): pl.pallas_call(functools.partial(place_kernel, parts, takes), out_shape=j...  0.73 us
  transfers between devices with their start and end apart: 7, of which 5 were waited for; matrix products, arithmetic and copies ran while one was open for 0% of the time, Pallas kernels for 10%

profile of v5, /device:TPU:0, one launch (start us, length us, event | category | flops | bytes accessed | tf_op | source)
XLA Modules:
  0.0 22.1 jit_solution(17793871959720508565)
XLA Ops:
  0.0 0.0 copy-start
  0.0 0.0 copy-start.1
  0.0 2.9 %collective-permute-start = (bf16[320,128]{1,0:T(8,128)(2,1)}, bf16[320,128]{1,0:T(8,128)(2,1)S(1)}, u32[]{:S(2)}, u32[]{:S(2)}) collective-permute-start(bf16[320,128]{1,0:T(8,128)(2,1)} %own_ref.1), channel_id=1, source_target_pairs={{0,2},{2,4},{4,6},{6,8},{8,10},{10,12},{12,14},{14,16},{16,18},{18... | collective-permute-start | bytes 245768 | tf_op jit(solution)/shard_map/ppermute | solution.py:166
  2.9 4.1 %collective-permute-start.1 = (bf16[320,128]{1,0:T(8,128)(2,1)}, bf16[320,128]{1,0:T(8,128)(2,1)S(1)}, u32[]{:S(2)}, u32[]{:S(2)}) collective-permute-start(bf16[320,128]{1,0:T(8,128)(2,1)} %own_ref.1), channel_id=1, source_target_pairs={{0,30},{2,0},{4,2},{6,4},{8,6},{10,8},{12,10},{14,12},{16,14},{18,... | collective-permute-start | bytes 245768 | tf_op jit(solution)/shard_map/ppermute | solution.py:166
  7.0 2.2 %shard_map.46.three_ref = bf16[4,64,64,128]{3,2,1,0:T(8,128)(2,1)S(1)} custom-call(bf16[4,64,64,128]{3,2,1,0:T(8,128)(2,1)} %source.1), custom_call_target="tpu_custom_call" | custom-call | tf_op jit(solution)/shard_map/pallas_call | solution.py:174
  9.2 0.0 copy-start.2
  9.2 0.5 %collective-permute-done.near_ref = bf16[320,128]{1,0:T(8,128)(2,1)S(1)} collective-permute-done((bf16[320,128]{1,0:T(8,128)(2,1)}, bf16[320,128]{1,0:T(8,128)(2,1)S(1)}, u32[]{:S(2)}, u32[]{:S(2)}) %collective-permute-start) | collective-permute-done | bytes 81952 | tf_op jit(solution)/shard_map/ppermute | solution.py:166
  9.8 0.0 collective-permute-done.1.far_ref
  9.8 0.0 copy-done
  9.8 0.0 copy-done.1
  9.8 3.0 %shard_map.47 = (f32[3,4,16,128]{3,2,1,0:T(8,128)S(1)}, f32[3,4,16,128]{3,2,1,0:T(8,128)S(1)}, f32[4,16,128]{2,1,0:T(8,128)S(1)}, f32[4,16,128]{2,1,0:T(8,128)S(1)}) custom-call(s32[2,4]{1,0:T(2,128)S(1)} %bitcast.2, bf16[320,128]{1,0:T(8,128)(2,1)S(1)} %collective-permute-done.near_ref, bf16[320,128]{1,0:T(8,128)(2,1)S(1)} %copy-done, ...), custom_call_target="tpu_custom_call" | custom-call | tf_op jit(solution)/shard_map/pallas_call | solution.py:182
  12.8 0.1 collective-permute-start.3
  12.8 0.5 %collective-permute-start.2 = (f32[4,16,128]{2,1,0:T(8,128)S(1)}, f32[4,16,128]{2,1,0:T(8,128)S(1)}, u32[]{:S(2)}, u32[]{:S(2)}) collective-permute-start(f32[4,16,128]{2,1,0:T(8,128)S(1)} %get-tuple-element.13), channel_id=1, source_target_pairs={{0,1},{1,0},{2,3},{3,2},{4,5},{5,4},{6,7},{7,6},{8,9},{9,8},{10,11... | collective-permute-start | bytes 98312 | tf_op jit(solution)/shard_map/ppermute | solution.py:166
  13.3 0.8 %collective-permute-done.3.refs_1_ = f32[3,4,16,128]{3,2,1,0:T(8,128)S(1)} collective-permute-done((f32[3,4,16,128]{3,2,1,0:T(8,128)S(1)}, f32[3,4,16,128]{3,2,1,0:T(8,128)S(1)}, u32[]{:S(2)}, u32[]{:S(2)}) %collective-permute-start.3) | collective-permute-done | bytes 98336 | tf_op jit(solution)/shard_map/ppermute | solution.py:166
  14.2 1.4 %collective-permute-start.4 = (f32[4,16,128]{2,1,0:T(8,128)S(1)}, f32[4,16,128]{2,1,0:T(8,128)S(1)}, u32[]{:S(2)}, u32[]{:S(2)}) collective-permute-start(f32[4,16,128]{2,1,0:T(8,128)S(1)} %get-tuple-element.16), channel_id=1, source_target_pairs={{0,16},{2,18},{4,20},{6,4},{8,24},{10,8},{12,10},{14,22},{16,14},{... | collective-permute-start | bytes 98312 | tf_op jit(solution)/shard_map/ppermute | solution.py:208
  15.6 1.6 %collective-permute-start.5 = (f32[4,16,128]{2,1,0:T(8,128)S(1)}, f32[4,16,128]{2,1,0:T(8,128)S(1)}, u32[]{:S(2)}, u32[]{:S(2)}) collective-permute-start(f32[4,16,128]{2,1,0:T(8,128)S(1)} %get-tuple-element.17), channel_id=1, source_target_pairs={{0,8},{2,10},{4,12},{6,14},{8,16},{10,26},{12,20},{14,30},{16,0},{... | collective-permute-start | bytes 98312 | tf_op jit(solution)/shard_map/ppermute | solution.py:208
  17.2 2.7 %collective-permute-start.6 = (f32[4,16,128]{2,1,0:T(8,128)S(1)}, f32[4,16,128]{2,1,0:T(8,128)S(1)}, u32[]{:S(2)}, u32[]{:S(2)}) collective-permute-start(f32[4,16,128]{2,1,0:T(8,128)S(1)} %get-tuple-element.18), channel_id=1, source_target_pairs={{0,30},{2,0},{4,2},{6,22},{8,6},{10,18},{12,28},{14,12},{16,24},{1... | collective-permute-start | bytes 98312 | tf_op jit(solution)/shard_map/ppermute | solution.py:208
  19.8 0.0 collective-permute-done.2.refs_1_
  19.8 0.2 collective-permute-done.4.refs_2_
  20.0 1.2 %collective-permute-done.5.refs_3_ = f32[4,16,128]{2,1,0:T(8,128)S(1)} collective-permute-done((f32[4,16,128]{2,1,0:T(8,128)S(1)}, f32[4,16,128]{2,1,0:T(8,128)S(1)}, u32[]{:S(2)}, u32[]{:S(2)}) %collective-permute-start.5) | collective-permute-done | bytes 32800 | tf_op jit(solution)/shard_map/ppermute | solution.py:208
  21.2 0.2 collective-permute-done.6.refs_4_
  21.4 0.0 copy-done.2
  21.4 0.7 %shard_map.49 = f32[7,2048]{1,0:T(8,128)} custom-call(s32[1,112]{1,0:T(1,128)S(1)} %bitcast.3, f32[4,16,128]{2,1,0:T(8,128)S(1)} %get-tuple-element.12.refs_0_, f32[4,16,128]{2,1,0:T(8,128)S(1)} %collective-permute-done.2.refs_1_, f32[4,16,128]{2,1,0:T(8,128)S(1)} %collective-permute-done.4.refs_2_, f32[4,16,128]{2,1,0:T(8,128)S(1)} %collective-permute-done.5.refs_3_, ...), custom_call_target="tpu_custom_call" | custom-call | tf_op jit(solution)/shard_map/pallas_call | solution.py:210
  (1 shorter events, 0.0 us)
Async XLA Ops:
  0.0 9.8 %copy-start = (bf16[320,128]{1,0:T(8,128)(2,1)S(1)}, bf16[320,128]{1,0:T(8,128)(2,1)}, u32[]{:S(2)}) copy-start(bf16[320,128]{1,0:T(8,128)(2,1)} %own_ref.1) | copy-start | bytes 245764
  0.0 9.8 %copy-start.1 = (s32[4,2]{0,1:T(2,128)S(1)}, s32[4,2]{0,1:T(2,128)}, u32[]{:S(2)}) copy-start(s32[4,2]{0,1:T(2,128)} %param.7) | copy-start | bytes 100
  0.0 9.8 %collective-permute-start = (bf16[320,128]{1,0:T(8,128)(2,1)}, bf16[320,128]{1,0:T(8,128)(2,1)S(1)}, u32[]{:S(2)}, u32[]{:S(2)}) collective-permute-start(bf16[320,128]{1,0:T(8,128)(2,1)} %own_ref.1), channel_id=1, source_target_pairs={{0,2},{2,4},{4,6},{6,8},{8,10},{10,12},{12,14},{14,16},{16,18},{18... | collective-permute-start | bytes 245768 | tf_op jit(solution)/shard_map/ppermute | solution.py:166
  2.9 6.8 %collective-permute-start.1 = (bf16[320,128]{1,0:T(8,128)(2,1)}, bf16[320,128]{1,0:T(8,128)(2,1)S(1)}, u32[]{:S(2)}, u32[]{:S(2)}) collective-permute-start(bf16[320,128]{1,0:T(8,128)(2,1)} %own_ref.1), channel_id=1, source_target_pairs={{0,30},{2,0},{4,2},{6,4},{8,6},{10,8},{12,10},{14,12},{16,14},{18,... | collective-permute-start | bytes 245768 | tf_op jit(solution)/shard_map/ppermute | solution.py:166
  9.2 12.2 %copy-start.2 = (s32[112]{0:T(128)S(1)}, s32[112]{0:T(128)}, u32[]{:S(2)}) copy-start(s32[112]{0:T(128)} %param.8) | copy-start | bytes 1348
  12.8 1.4 %collective-permute-start.3 = (f32[3,4,16,128]{3,2,1,0:T(8,128)S(1)}, f32[3,4,16,128]{3,2,1,0:T(8,128)S(1)}, u32[]{:S(2)}, u32[]{:S(2)}) collective-permute-start(f32[3,4,16,128]{3,2,1,0:T(8,128)S(1)} %get-tuple-element.15), channel_id=1, source_target_pairs={{0,1},{1,0},{2,3},{3,2},{4,5},{5,4},{6,7},{7,6},{8,9},{9,8},{10,11... | collective-permute-start | bytes 294920 | tf_op jit(solution)/shard_map/ppermute | solution.py:166
  12.8 7.0 %collective-permute-start.2 = (f32[4,16,128]{2,1,0:T(8,128)S(1)}, f32[4,16,128]{2,1,0:T(8,128)S(1)}, u32[]{:S(2)}, u32[]{:S(2)}) collective-permute-start(f32[4,16,128]{2,1,0:T(8,128)S(1)} %get-tuple-element.13), channel_id=1, source_target_pairs={{0,1},{1,0},{2,3},{3,2},{4,5},{5,4},{6,7},{7,6},{8,9},{9,8},{10,11... | collective-permute-start | bytes 98312 | tf_op jit(solution)/shard_map/ppermute | solution.py:166
  14.2 5.9 %collective-permute-start.4 = (f32[4,16,128]{2,1,0:T(8,128)S(1)}, f32[4,16,128]{2,1,0:T(8,128)S(1)}, u32[]{:S(2)}, u32[]{:S(2)}) collective-permute-start(f32[4,16,128]{2,1,0:T(8,128)S(1)} %get-tuple-element.16), channel_id=1, source_target_pairs={{0,16},{2,18},{4,20},{6,4},{8,24},{10,8},{12,10},{14,22},{16,14},{... | collective-permute-start | bytes 98312 | tf_op jit(solution)/shard_map/ppermute | solution.py:208
  15.6 5.7 %collective-permute-start.5 = (f32[4,16,128]{2,1,0:T(8,128)S(1)}, f32[4,16,128]{2,1,0:T(8,128)S(1)}, u32[]{:S(2)}, u32[]{:S(2)}) collective-permute-start(f32[4,16,128]{2,1,0:T(8,128)S(1)} %get-tuple-element.17), channel_id=1, source_target_pairs={{0,8},{2,10},{4,12},{6,14},{8,16},{10,26},{12,20},{14,30},{16,0},{... | collective-permute-start | bytes 98312 | tf_op jit(solution)/shard_map/ppermute | solution.py:208
  17.2 4.3 %collective-permute-start.6 = (f32[4,16,128]{2,1,0:T(8,128)S(1)}, f32[4,16,128]{2,1,0:T(8,128)S(1)}, u32[]{:S(2)}, u32[]{:S(2)}) collective-permute-start(f32[4,16,128]{2,1,0:T(8,128)S(1)} %get-tuple-element.18), channel_id=1, source_target_pairs={{0,30},{2,0},{4,2},{6,22},{8,6},{10,18},{12,28},{14,12},{16,24},{1... | collective-permute-start | bytes 98312 | tf_op jit(solution)/shard_map/ppermute | solution.py:208

commit v6 on v5

--- a/solution.py
+++ b/solution.py
@@ -15,6 +15,7 @@
         [15, 0, 1, 11, 3, 9, 14, 6, 12, 8, 2, 10, 4, 5, 13, 7],
     ],
 }
+SLOTS = 8
 CHUNK = 8
 VMEM = pl.BlockSpec(memory_space=pltpu.VMEM)
 SMEM = pl.BlockSpec(memory_space=pltpu.SMEM)
@@ -56,29 +57,41 @@
             at = (e % 2) * depth + t * block
             sel[e // 2, at : at + block, (e % 2) * orbitals : (e % 2 + 1) * orbitals] = rows
 
-    acc[...] = jnp.zeros_like(acc)
-
-    def step(s, carry):
-        start = pl.multiple_of(s * CHUNK, CHUNK)
+    def transform(s):
         for pair in range(entries // 2):
             lhs = jnp.concatenate(
-                [three_ref[2 * pair + i, pl.ds(start, CHUNK)].reshape(CHUNK * block, depth) for i in range(2)], axis=1
+                [
+                    three_ref[2 * pair + i, s * CHUNK : (s + 1) * CHUNK].reshape(CHUNK * block, depth)
+                    for i in range(2)
+                ],
+                axis=1,
             )
             res = jnp.dot(lhs, sel[pair], preferred_element_type=jnp.float32).astype(jnp.bfloat16)
             for i in range(2):
                 e = 2 * pair + i
                 for p in range(CHUNK):
-                    half[e * block : (e + 1) * block, p * orbitals : (p + 1) * orbitals] = res[
+                    half[s % SLOTS, e * block : (e + 1) * block, p * orbitals : (p + 1) * orbitals] = res[
                         p * block : (p + 1) * block, i * orbitals : (i + 1) * orbitals
                     ]
-        full = half[...]
-        acc[...] += lax.dot_general(full, full, (((1,), (1,)), ((), ())), preferred_element_type=jnp.float32)
-        return carry
-
-    lax.fori_loop(0, aux_count // CHUNK, step, 0, unroll=True)
-
-    for h in range(entries // 2):
-        panels[h] = acc[:, h * LANES : (h + 1) * LANES]
+
+    def gather(s):
+        full = half[s % SLOTS]
+        value = lax.dot_general(full, full, (((1,), (1,)), ((), ())), preferred_element_type=jnp.float32)
+        if s == 0:
+            acc[...] = value
+        elif s < aux_count // CHUNK - 1:
+            acc[...] += value
+        else:
+            value = acc[...] + value
+            for h in range(entries // 2):
+                panels[h] = value[:, h * LANES : (h + 1) * LANES]
+
+    transform(0)
+    for s in range(1, aux_count // CHUNK):
+        transform(s)
+        gather(s - 1)
+    gather(aux_count // CHUNK - 1)
+
     count = block * block // parts // LANES
     low = lax.broadcasted_iota(jnp.int32, (count, LANES), 1) < block
     for r in range(parts):
@@ -188,11 +201,11 @@
         scratch_shapes=[
             pltpu.VMEM((3 * shard_rows, orbitals), jnp.bfloat16),
             pltpu.VMEM((entries // 2, 2 * depth, 2 * orbitals), jnp.bfloat16),
-            pltpu.VMEM((entries * block, CHUNK * orbitals), jnp.bfloat16),
+            pltpu.VMEM((SLOTS, entries * block, CHUNK * orbitals), jnp.bfloat16),
             pltpu.VMEM((entries * block, entries * block), jnp.float32),
             pltpu.VMEM((entries // 2, entries * block, LANES), jnp.float32),
         ],
-        compiler_params=pltpu.CompilerParams(vmem_limit_bytes=12 * 1024 * 1024),
+        compiler_params=pltpu.CompilerParams(vmem_limit_bytes=16 * 1024 * 1024),
     )(basis_blocks.T, neighbour, coefficients, other, held)
     terms = [pieces[0]] + [shift(pieces[r], "occ", r) for r in range(1, parts)]
     targets, sends, takes = route(groups, entries)

time: 22.4 us -> 22.4 us (level)
  no operation moved by 1% of the time
where the time goes in v6:
time: 22.4 us; the launch traced here: 22.1 us
  starting transfers between devices  13.2 us (59%)
  Pallas kernels  5.93 us (26%)
  waiting for transfers between devices  2.93 us (13%)
    ppermute x4, starting transfers between devices, shift(): lax.ppermute(value, axis, [(i, (i + by) % size) for i in range(size)])  7.56 us
    ppermute x3, starting transfers between devices, per_device(): moved.append(lax.ppermute(value, 'aux', list(enumerate(each))))  5.65 us
    pallas_call x1, Pallas kernels, per_device(): pl.pallas_call(functools.partial(build_kernel, groups, parts), out_shape=...  2.99 us
    pallas_call x1, Pallas kernels, per_device(): pl.pallas_call(fetch_kernel, out_shape=jax.ShapeDtypeStruct(three_index.s...  2.2 us
    ppermute x3, waiting for transfers between devices, per_device(): moved.append(lax.ppermute(value, 'aux', list(enumerate(each))))  1.59 us
    ppermute x4, waiting for transfers between devices, shift(): lax.ppermute(value, axis, [(i, (i + by) % size) for i in range(size)])  1.34 us
    pallas_call x1, Pallas kernels, per_device(): pl.pallas_call(functools.partial(place_kernel, parts, takes), out_shape=j...  0.73 us
  transfers between devices with their start and end apart: 7, of which 5 were waited for; matrix products, arithmetic and copies ran while one was open for 0% of the time, Pallas kernels for 10%

profile of v6, /device:TPU:0, one launch (start us, length us, event | category | flops | bytes accessed | tf_op | source)
XLA Modules:
  0.0 22.1 jit_solution(1299344334706451093)
XLA Ops:
  0.0 0.0 copy-start
  0.0 0.0 copy-start.1
  0.0 2.9 %collective-permute-start = (bf16[320,128]{1,0:T(8,128)(2,1)}, bf16[320,128]{1,0:T(8,128)(2,1)S(1)}, u32[]{:S(2)}, u32[]{:S(2)}) collective-permute-start(bf16[320,128]{1,0:T(8,128)(2,1)} %own_ref.1), channel_id=1, source_target_pairs={{0,2},{2,4},{4,6},{6,8},{8,10},{10,12},{12,14},{14,16},{16,18},{18... | collective-permute-start | bytes 245768 | tf_op jit(solution)/shard_map/ppermute | solution.py:179
  2.9 4.1 %collective-permute-start.1 = (bf16[320,128]{1,0:T(8,128)(2,1)}, bf16[320,128]{1,0:T(8,128)(2,1)S(1)}, u32[]{:S(2)}, u32[]{:S(2)}) collective-permute-start(bf16[320,128]{1,0:T(8,128)(2,1)} %own_ref.1), channel_id=1, source_target_pairs={{0,30},{2,0},{4,2},{6,4},{8,6},{10,8},{12,10},{14,12},{16,14},{18,... | collective-permute-start | bytes 245768 | tf_op jit(solution)/shard_map/ppermute | solution.py:179
  7.0 2.2 %shard_map.46.three_ref = bf16[4,64,64,128]{3,2,1,0:T(8,128)(2,1)S(1)} custom-call(bf16[4,64,64,128]{3,2,1,0:T(8,128)(2,1)} %source.1), custom_call_target="tpu_custom_call" | custom-call | tf_op jit(solution)/shard_map/pallas_call | solution.py:187
  9.2 0.0 copy-start.2
  9.2 0.5 %collective-permute-done.near_ref = bf16[320,128]{1,0:T(8,128)(2,1)S(1)} collective-permute-done((bf16[320,128]{1,0:T(8,128)(2,1)}, bf16[320,128]{1,0:T(8,128)(2,1)S(1)}, u32[]{:S(2)}, u32[]{:S(2)}) %collective-permute-start) | collective-permute-done | bytes 81952 | tf_op jit(solution)/shard_map/ppermute | solution.py:179
  9.8 0.0 collective-permute-done.1.far_ref
  9.8 0.0 copy-done
  9.8 0.0 copy-done.1
  9.8 3.0 %shard_map.47 = (f32[3,4,16,128]{3,2,1,0:T(8,128)S(1)}, f32[3,4,16,128]{3,2,1,0:T(8,128)S(1)}, f32[4,16,128]{2,1,0:T(8,128)S(1)}, f32[4,16,128]{2,1,0:T(8,128)S(1)}) custom-call(s32[2,4]{1,0:T(2,128)S(1)} %bitcast.2, bf16[320,128]{1,0:T(8,128)(2,1)S(1)} %collective-permute-done.near_ref, bf16[320,128]{1,0:T(8,128)(2,1)S(1)} %copy-done, ...), custom_call_target="tpu_custom_call" | custom-call | tf_op jit(solution)/shard_map/pallas_call | solution.py:195
  12.8 0.1 collective-permute-start.3
  12.8 0.5 %collective-permute-start.2 = (f32[4,16,128]{2,1,0:T(8,128)S(1)}, f32[4,16,128]{2,1,0:T(8,128)S(1)}, u32[]{:S(2)}, u32[]{:S(2)}) collective-permute-start(f32[4,16,128]{2,1,0:T(8,128)S(1)} %get-tuple-element.13), channel_id=1, source_target_pairs={{0,1},{1,0},{2,3},{3,2},{4,5},{5,4},{6,7},{7,6},{8,9},{9,8},{10,11... | collective-permute-start | bytes 98312 | tf_op jit(solution)/shard_map/ppermute | solution.py:179
  13.3 0.8 %collective-permute-done.3.refs_1_ = f32[3,4,16,128]{3,2,1,0:T(8,128)S(1)} collective-permute-done((f32[3,4,16,128]{3,2,1,0:T(8,128)S(1)}, f32[3,4,16,128]{3,2,1,0:T(8,128)S(1)}, u32[]{:S(2)}, u32[]{:S(2)}) %collective-permute-start.3) | collective-permute-done | bytes 98336 | tf_op jit(solution)/shard_map/ppermute | solution.py:179
  14.2 1.4 %collective-permute-start.4 = (f32[4,16,128]{2,1,0:T(8,128)S(1)}, f32[4,16,128]{2,1,0:T(8,128)S(1)}, u32[]{:S(2)}, u32[]{:S(2)}) collective-permute-start(f32[4,16,128]{2,1,0:T(8,128)S(1)} %get-tuple-element.16), channel_id=1, source_target_pairs={{0,16},{2,18},{4,20},{6,4},{8,24},{10,8},{12,10},{14,22},{16,14},{... | collective-permute-start | bytes 98312 | tf_op jit(solution)/shard_map/ppermute | solution.py:221
  15.6 1.6 %collective-permute-start.5 = (f32[4,16,128]{2,1,0:T(8,128)S(1)}, f32[4,16,128]{2,1,0:T(8,128)S(1)}, u32[]{:S(2)}, u32[]{:S(2)}) collective-permute-start(f32[4,16,128]{2,1,0:T(8,128)S(1)} %get-tuple-element.17), channel_id=1, source_target_pairs={{0,8},{2,10},{4,12},{6,14},{8,16},{10,26},{12,20},{14,30},{16,0},{... | collective-permute-start | bytes 98312 | tf_op jit(solution)/shard_map/ppermute | solution.py:221
  17.2 2.7 %collective-permute-start.6 = (f32[4,16,128]{2,1,0:T(8,128)S(1)}, f32[4,16,128]{2,1,0:T(8,128)S(1)}, u32[]{:S(2)}, u32[]{:S(2)}) collective-permute-start(f32[4,16,128]{2,1,0:T(8,128)S(1)} %get-tuple-element.18), channel_id=1, source_target_pairs={{0,30},{2,0},{4,2},{6,22},{8,6},{10,18},{12,28},{14,12},{16,24},{1... | collective-permute-start | bytes 98312 | tf_op jit(solution)/shard_map/ppermute | solution.py:221
  19.8 0.0 collective-permute-done.2.refs_1_
  19.8 0.2 collective-permute-done.4.refs_2_
  20.0 1.2 %collective-permute-done.5.refs_3_ = f32[4,16,128]{2,1,0:T(8,128)S(1)} collective-permute-done((f32[4,16,128]{2,1,0:T(8,128)S(1)}, f32[4,16,128]{2,1,0:T(8,128)S(1)}, u32[]{:S(2)}, u32[]{:S(2)}) %collective-permute-start.5) | collective-permute-done | bytes 32800 | tf_op jit(solution)/shard_map/ppermute | solution.py:221
  21.2 0.2 collective-permute-done.6.refs_4_
  21.4 0.0 copy-done.2
  21.4 0.7 %shard_map.49 = f32[7,2048]{1,0:T(8,128)} custom-call(s32[1,112]{1,0:T(1,128)S(1)} %bitcast.3, f32[4,16,128]{2,1,0:T(8,128)S(1)} %get-tuple-element.12.refs_0_, f32[4,16,128]{2,1,0:T(8,128)S(1)} %collective-permute-done.2.refs_1_, f32[4,16,128]{2,1,0:T(8,128)S(1)} %collective-permute-done.4.refs_2_, f32[4,16,128]{2,1,0:T(8,128)S(1)} %collective-permute-done.5.refs_3_, ...), custom_call_target="tpu_custom_call" | custom-call | tf_op jit(solution)/shard_map/pallas_call | solution.py:223
  (1 shorter events, 0.0 us)
Async XLA Ops:
  0.0 9.8 %copy-start = (bf16[320,128]{1,0:T(8,128)(2,1)S(1)}, bf16[320,128]{1,0:T(8,128)(2,1)}, u32[]{:S(2)}) copy-start(bf16[320,128]{1,0:T(8,128)(2,1)} %own_ref.1) | copy-start | bytes 245764
  0.0 9.8 %copy-start.1 = (s32[4,2]{0,1:T(2,128)S(1)}, s32[4,2]{0,1:T(2,128)}, u32[]{:S(2)}) copy-start(s32[4,2]{0,1:T(2,128)} %param.7) | copy-start | bytes 100
  0.0 9.8 %collective-permute-start = (bf16[320,128]{1,0:T(8,128)(2,1)}, bf16[320,128]{1,0:T(8,128)(2,1)S(1)}, u32[]{:S(2)}, u32[]{:S(2)}) collective-permute-start(bf16[320,128]{1,0:T(8,128)(2,1)} %own_ref.1), channel_id=1, source_target_pairs={{0,2},{2,4},{4,6},{6,8},{8,10},{10,12},{12,14},{14,16},{16,18},{18... | collective-permute-start | bytes 245768 | tf_op jit(solution)/shard_map/ppermute | solution.py:179
  2.9 6.8 %collective-permute-start.1 = (bf16[320,128]{1,0:T(8,128)(2,1)}, bf16[320,128]{1,0:T(8,128)(2,1)S(1)}, u32[]{:S(2)}, u32[]{:S(2)}) collective-permute-start(bf16[320,128]{1,0:T(8,128)(2,1)} %own_ref.1), channel_id=1, source_target_pairs={{0,30},{2,0},{4,2},{6,4},{8,6},{10,8},{12,10},{14,12},{16,14},{18,... | collective-permute-start | bytes 245768 | tf_op jit(solution)/shard_map/ppermute | solution.py:179
  9.2 12.2 %copy-start.2 = (s32[112]{0:T(128)S(1)}, s32[112]{0:T(128)}, u32[]{:S(2)}) copy-start(s32[112]{0:T(128)} %param.8) | copy-start | bytes 1348
  12.8 1.4 %collective-permute-start.3 = (f32[3,4,16,128]{3,2,1,0:T(8,128)S(1)}, f32[3,4,16,128]{3,2,1,0:T(8,128)S(1)}, u32[]{:S(2)}, u32[]{:S(2)}) collective-permute-start(f32[3,4,16,128]{3,2,1,0:T(8,128)S(1)} %get-tuple-element.15), channel_id=1, source_target_pairs={{0,1},{1,0},{2,3},{3,2},{4,5},{5,4},{6,7},{7,6},{8,9},{9,8},{10,11... | collective-permute-start | bytes 294920 | tf_op jit(solution)/shard_map/ppermute | solution.py:179
  12.8 7.0 %collective-permute-start.2 = (f32[4,16,128]{2,1,0:T(8,128)S(1)}, f32[4,16,128]{2,1,0:T(8,128)S(1)}, u32[]{:S(2)}, u32[]{:S(2)}) collective-permute-start(f32[4,16,128]{2,1,0:T(8,128)S(1)} %get-tuple-element.13), channel_id=1, source_target_pairs={{0,1},{1,0},{2,3},{3,2},{4,5},{5,4},{6,7},{7,6},{8,9},{9,8},{10,11... | collective-permute-start | bytes 98312 | tf_op jit(solution)/shard_map/ppermute | solution.py:179
  14.2 5.9 %collective-permute-start.4 = (f32[4,16,128]{2,1,0:T(8,128)S(1)}, f32[4,16,128]{2,1,0:T(8,128)S(1)}, u32[]{:S(2)}, u32[]{:S(2)}) collective-permute-start(f32[4,16,128]{2,1,0:T(8,128)S(1)} %get-tuple-element.16), channel_id=1, source_target_pairs={{0,16},{2,18},{4,20},{6,4},{8,24},{10,8},{12,10},{14,22},{16,14},{... | collective-permute-start | bytes 98312 | tf_op jit(solution)/shard_map/ppermute | solution.py:221
  15.6 5.7 %collective-permute-start.5 = (f32[4,16,128]{2,1,0:T(8,128)S(1)}, f32[4,16,128]{2,1,0:T(8,128)S(1)}, u32[]{:S(2)}, u32[]{:S(2)}) collective-permute-start(f32[4,16,128]{2,1,0:T(8,128)S(1)} %get-tuple-element.17), channel_id=1, source_target_pairs={{0,8},{2,10},{4,12},{6,14},{8,16},{10,26},{12,20},{14,30},{16,0},{... | collective-permute-start | bytes 98312 | tf_op jit(solution)/shard_map/ppermute | solution.py:221
  17.2 4.3 %collective-permute-start.6 = (f32[4,16,128]{2,1,0:T(8,128)S(1)}, f32[4,16,128]{2,1,0:T(8,128)S(1)}, u32[]{:S(2)}, u32[]{:S(2)}) collective-permute-start(f32[4,16,128]{2,1,0:T(8,128)S(1)} %get-tuple-element.18), channel_id=1, source_target_pairs={{0,30},{2,0},{4,2},{6,22},{8,6},{10,18},{12,28},{14,12},{16,24},{1... | collective-permute-start | bytes 98312 | tf_op jit(solution)/shard_map/ppermute | solution.py:221
